TPU v7x, 32 devices: a whole 2x2x4 slice. The times are simulated.
32 devices in a mesh: img: 8 (over y, x, core), row: 4 (over z).
Axes of the slice: x: 2, y: 2, z: 4, core: 2. Of those that a mesh axis runs over, the one named last changes fastest.
Arguments:
- images: bfloat16 [8, 20, 96, 512], P('img', 'row'), may hold values from -6 to 6
- cotangent: bfloat16 [8, 20, 96, 512], P('img', 'row'), may hold values from -6 to 6
- params: bfloat16 [2, 3111680], P(None, ('img', 'row')), may hold values from -2 to 2, as said below
- heights: int32 [8], P('img'), may hold values from 18 to 20, as said below
- widths: int32 [8], P('img'), may hold values from 48 to 96, as said below
Outputs:
- outputs: bfloat16 [8, 20, 96, 512], P('img', 'row')
- input_grad: bfloat16 [8, 20, 96, 512], P('img', 'row')
- param_grads: float32 [2, 3111680], P(None, ('img', 'row'))
Inputs may be any that keep to these rules, and one draw needn't show every extreme that they name: `params`: zero in each block's padding beyond 3111680. `heights`: one image has all 20 rows and one has 18. `widths`: one image has all 96 columns and one has 48.
All inputs are finite; a program needn't handle non-finite values.
Results may differ from a plain program's by a relative error of at most 0.025.
Values may be sent and summed in bfloat16 or wider, within the bound.
A program may use at most 192 MiB of HBM per device.

v0:
```python
import math

import jax
import jax.numpy as jnp
from jax import lax
from jax.sharding import PartitionSpec as P

THIRD = 1.0 / 3.0


def padded_2(x, sides, width):
    for axis, dim in sides:
        size, length = (lax.axis_size(axis), x.shape[dim])
        up = [(i, (i + 1) % size) for i in range(size - 1)]
        down = [(j, i) for i, j in up]
        last = lax.slice_in_dim(x, length - width, length, axis=dim)
        leading = lax.slice_in_dim(x, 0, width, axis=dim)
        before = lax.ppermute(last, axis, up)
        after = lax.ppermute(leading, axis, down)
        x = jnp.concatenate([before, x, after], axis=dim)
    return x


def layout(width):
    first = width // 8
    mixed = 15 * width // 8
    return [
        ("norm_gain", (width,)),
        ("norm_shift", (width,)),
        ("inner_weight", (width, 2 * width)),
        ("inner_bias", (2 * width,)),
        ("kernel", (7, 7, mixed)),
        ("kernel_bias", (mixed,)),
        ("order_one", (first, 2 * first)),
        ("bias_one", (2 * first,)),
        ("order_two", (2 * first, 4 * first)),
        ("bias_two", (4 * first,)),
        ("order_three", (4 * first, 8 * first)),
        ("bias_three", (8 * first,)),
        ("outer_weight", (width, width)),
        ("outer_bias", (width,)),
        ("scale_mixer", (width,)),
        ("second_gain", (width,)),
        ("second_shift", (width,)),
        ("expand", (width, 4 * width)),
        ("expand_bias", (4 * width,)),
        ("reduce", (4 * width, width)),
        ("reduce_bias", (width,)),
        ("scale_mlp", (width,)),
    ]


def unpack(flat, width):
    pieces = {}
    offset = 0
    for name, shape in layout(width):
        count = math.prod(shape)
        pieces[name] = flat[offset : offset + count].reshape(shape)
        offset = offset + count
    return pieces


def as_float(value):
    return value.astype(jnp.float32)


def product(left, right):
    return jnp.dot(left, right, preferred_element_type=jnp.float32)


def back_product(grad, weight):
    return lax.dot_general(
        grad, weight, (((grad.ndim - 1,), (1,)), ((), ())), preferred_element_type=jnp.float32
    )


def outer_sum(left, grad):
    return lax.dot_general(
        left.reshape(-1, left.shape[-1]),
        grad.reshape(-1, grad.shape[-1]),
        (((0,), (0,)), ((), ())),
        preferred_element_type=jnp.float32,
    )


def pixel_sum(value):
    return jnp.sum(as_float(value), axis=(0, 1, 2))


def layer_norm(values, gain, shift):
    mean = jnp.mean(values, -1, keepdims=True)
    centered = values - mean
    inverse = lax.rsqrt(jnp.mean(centered * centered, -1, keepdims=True) + 1e-06)
    normal = centered * inverse
    return (normal * gain + shift, normal, inverse)


def norm_back(grad_normed, normal, inverse, gain):
    scaled = grad_normed * gain
    return inverse * (
        scaled
        - jnp.mean(scaled, -1, keepdims=True)
        - normal * jnp.mean(scaled * normal, -1, keepdims=True)
    )


def taps(padded, kernel, rows, cols):
    total = jnp.zeros(padded.shape[:1] + (rows, cols, padded.shape[-1]), jnp.float32)
    for row in range(7):
        for col in range(7):
            total = (
                total
                + as_float(padded[:, row : row + rows, col : col + cols, :]) * kernel[row, col]
            )
    return total


def pad_columns(field):
    return jnp.pad(field, ((0, 0), (0, 0), (3, 3), (0, 0)))


def front(values, weights, valid, first):
    normed, normal, inverse = layer_norm(
        values, as_float(weights["norm_gain"]), as_float(weights["norm_shift"])
    )
    normed_low = normed.astype(jnp.bfloat16)
    inner = product(normed_low, weights["inner_weight"]) + as_float(weights["inner_bias"])
    rest = (inner[..., first:] * valid[..., None]).astype(jnp.bfloat16)
    return (normed_low, normal, inverse, inner, rest)


def mixer(values, weights, inner, padded, first, rows, cols):
    saved = {}
    mixed = (
        taps(padded, as_float(weights["kernel"]), rows, cols) + as_float(weights["kernel_bias"])
    ) * THIRD
    bounds = (0, first, 3 * first, 7 * first, 15 * first)
    gates = [mixed[..., bounds[index] : bounds[index + 1]] for index in range(4)]
    gated = inner[..., :first] * gates[0]
    chain = [gated]
    linear = []
    for name, bias in (
        ("order_one", "bias_one"),
        ("order_two", "bias_two"),
        ("order_three", "bias_three"),
    ):
        line = product(gated.astype(jnp.bfloat16), weights[name]) + as_float(weights[bias])
        linear.append(line)
        gated = line * gates[len(linear)]
        chain.append(gated)
    branch_mixer = product(gated.astype(jnp.bfloat16), weights["outer_weight"]) + as_float(
        weights["outer_bias"]
    )
    middle = values + as_float(weights["scale_mixer"]) * branch_mixer
    normed_second, normal_second, inverse_second = layer_norm(
        middle, as_float(weights["second_gain"]), as_float(weights["second_shift"])
    )
    normed_second = normed_second.astype(jnp.bfloat16)
    hidden = product(normed_second, weights["expand"]) + as_float(weights["expand_bias"])
    active = jax.nn.gelu(hidden, approximate=False).astype(jnp.bfloat16)
    branch_mlp = product(active, weights["reduce"]) + as_float(weights["reduce_bias"])
    result = middle + as_float(weights["scale_mlp"]) * branch_mlp
    saved["gates"] = gates
    saved["chain"] = chain
    saved["linear"] = linear
    saved["branch_mixer"] = branch_mixer
    saved["normal_second"] = normal_second
    saved["inverse_second"] = inverse_second
    saved["normed_second"] = normed_second
    saved["hidden"] = hidden
    saved["active"] = active
    saved["branch_mlp"] = branch_mlp
    return (result, saved)


def layer_back(
    grad_out, values, weights, padded, valid, first, rows, cols, total_length, front_kept, saved
):
    normed_low, normal, inverse, inner, rest = front_kept
    grads = {}
    grads["scale_mlp"] = jnp.sum(grad_out * saved["branch_mlp"], axis=(0, 1, 2))
    grad_branch = (grad_out * as_float(weights["scale_mlp"])).astype(jnp.bfloat16)
    grads["reduce_bias"] = pixel_sum(grad_branch)
    grads["reduce"] = outer_sum(saved["active"], grad_branch)
    grad_active = back_product(grad_branch, weights["reduce"])
    unused, gelu_pull = jax.vjp(
        lambda inside: jax.nn.gelu(inside, approximate=False), saved["hidden"]
    )
    grad_hidden = gelu_pull(grad_active)[0].astype(jnp.bfloat16)
    grads["expand_bias"] = pixel_sum(grad_hidden)
    grads["expand"] = outer_sum(saved["normed_second"], grad_hidden)
    grad_normed = back_product(grad_hidden, weights["expand"])
    grads["second_gain"] = jnp.sum(grad_normed * saved["normal_second"], axis=(0, 1, 2))
    grads["second_shift"] = jnp.sum(grad_normed, axis=(0, 1, 2))
    grad_middle = grad_out + norm_back(
        grad_normed,
        saved["normal_second"],
        saved["inverse_second"],
        as_float(weights["second_gain"]),
    )
    grads["scale_mixer"] = jnp.sum(grad_middle * saved["branch_mixer"], axis=(0, 1, 2))
    grad_branch = (grad_middle * as_float(weights["scale_mixer"])).astype(jnp.bfloat16)
    grads["outer_bias"] = pixel_sum(grad_branch)
    grads["outer_weight"] = outer_sum(saved["chain"][3].astype(jnp.bfloat16), grad_branch)
    grad_gated = back_product(grad_branch, weights["outer_weight"])
    gates = saved["gates"]
    grad_gates = [None, None, None, None]
    names = (("order_one", "bias_one"), ("order_two", "bias_two"), ("order_three", "bias_three"))
    for index in (2, 1, 0):
        grad_line = (grad_gated * gates[index + 1]).astype(jnp.bfloat16)
        grad_gates[index + 1] = grad_gated * saved["linear"][index]
        grads[names[index][1]] = pixel_sum(grad_line)
        grads[names[index][0]] = outer_sum(saved["chain"][index].astype(jnp.bfloat16), grad_line)
        grad_gated = back_product(grad_line, weights[names[index][0]])
    grad_gates[0] = grad_gated * inner[..., :first]
    grad_head = grad_gated * gates[0]
    grad_taps = (jnp.concatenate(grad_gates, -1) * THIRD).astype(jnp.bfloat16)
    grads["kernel_bias"] = pixel_sum(grad_taps)
    grad_float = as_float(grad_taps)
    kernel_rows = []
    for row in range(7):
        kernel_cols = []
        for col in range(7):
            kernel_cols.append(
                jnp.sum(
                    as_float(padded[:, row : row + rows, col : col + cols, :]) * grad_float,
                    axis=(0, 1, 2),
                )
            )
        kernel_rows.append(jnp.stack(kernel_cols))
    grads["kernel"] = jnp.stack(kernel_rows)
    grad_padded = pad_columns(padded_2(grad_taps, (("row", 1),), 3))
    kernel = as_float(weights["kernel"])
    grad_rest = jnp.zeros(grad_taps.shape, jnp.float32)
    for row in range(7):
        for col in range(7):
            grad_rest = (
                grad_rest
                + as_float(grad_padded[:, 6 - row : 6 - row + rows, 6 - col : 6 - col + cols, :])
                * kernel[row, col]
            )
    grad_inner = jnp.concatenate([grad_head, grad_rest * valid[..., None]], -1).astype(jnp.bfloat16)
    grads["inner_bias"] = pixel_sum(grad_inner)
    grads["inner_weight"] = outer_sum(normed_low, grad_inner)
    grad_first = back_product(grad_inner, weights["inner_weight"])
    grads["norm_gain"] = jnp.sum(grad_first * normal, axis=(0, 1, 2))
    grads["norm_shift"] = jnp.sum(grad_first, axis=(0, 1, 2))
    grad_values = grad_middle + norm_back(
        grad_first, normal, inverse, as_float(weights["norm_gain"])
    )
    flat_pieces = [grads[name].reshape(-1) for name, shape in layout(values.shape[-1])]
    used = sum((piece.shape[0] for piece in flat_pieces))
    flat_pieces.append(jnp.zeros((total_length - used,), jnp.float32))
    return (grad_values, jnp.concatenate(flat_pieces))


def body(images, cotangent, params, heights, widths):
    width = images.shape[-1]
    rows = images.shape[1]
    cols = images.shape[2]
    first = width // 8
    depth = params.shape[0]
    total_length = params.shape[1] * lax.axis_size(("img", "row"))
    image_count = lax.axis_size("img")
    line = lax.axis_index("row") * rows + jnp.arange(rows, dtype=jnp.int32)
    valid = (
        (line[:, None] < heights[0]) & (jnp.arange(cols, dtype=jnp.int32)[None, :] < widths[0])
    ).astype(jnp.float32)[None]
    values = images.astype(jnp.float32)
    kept_inputs = []
    kept_padded = []
    kept_weights = []
    kept_fronts = []
    kept_saved = []
    for layer in range(depth):
        gathered = lax.all_gather(params[layer], ("img", "row"), axis=0, tiled=True)
        weights = unpack(gathered, width)
        front_kept = front(values, weights, valid, first)
        padded = pad_columns(padded_2(front_kept[4], (("row", 1),), 3))
        kept_inputs.append(values)
        kept_padded.append(padded)
        kept_weights.append(weights)
        kept_fronts.append(front_kept)
        values, saved = mixer(values, weights, front_kept[3], padded, first, rows, cols)
        kept_saved.append(saved)
    outputs = values.astype(jnp.bfloat16)
    grad = cotangent.astype(jnp.float32)
    flat_grads = [None] * depth
    for layer in reversed(range(depth)):
        weights = unpack(lax.all_gather(params[layer], ("img", "row"), axis=0, tiled=True), width)
        grad, flat = layer_back(
            grad,
            kept_inputs[layer],
            weights,
            kept_padded[layer],
            valid,
            first,
            rows,
            cols,
            total_length,
            kept_fronts[layer],
            kept_saved[layer],
        )
        received = lax.all_to_all(
            flat.reshape(image_count, -1).astype(jnp.bfloat16),
            "img",
            split_axis=0,
            concat_axis=0,
            tiled=True,
        ).astype(jnp.float32)
        partial_sum = jnp.sum(received, 0)
        flat_grads[layer] = lax.psum_scatter(
            partial_sum.astype(jnp.bfloat16), "row", scatter_dimension=0, tiled=True
        ).astype(jnp.float32)
    summed = jnp.stack(flat_grads)
    return (outputs, grad.astype(jnp.bfloat16), summed)


def solution(mesh):
    return jax.shard_map(
        body,
        mesh=mesh,
        in_specs=(
            P("img", "row", None, None),
            P("img", "row", None, None),
            P(None, ("img", "row")),
            P("img"),
            P("img"),
        ),
        out_specs=(
            P("img", "row", None, None),
            P("img", "row", None, None),
            P(None, ("img", "row")),
        ),
        check_vma=False,
    )
```

profile of v0, /device:TPU:0, one launch (start us, length us, event | category | flops | bytes accessed | tf_op | source)
XLA Modules:
  0.0 1553.5 jit_solution(1216386345817096563)
XLA Ops:
  26.3 230.9 %all-reduce.13.cloned.1.call-done = (bf16[3111680]{0:T(1024)(128)(2,1)}, bf16[3111680]{0:T(1024)(128)(2,1)}) async-done(((bf16[3111680]{0:T(1024)(128)(2,1)}, bf16[3111680]{0:T(1024)(128)(2,1)}), (bf16[3111680]{0:T(1024)(128)(2,1)}, bf16[3111680]{0:T(1024)(128)(2,1)})) %all-reduce.13.cloned.1.call-update) | async-done | bytes 12446736
  257.2 60.4 %reshape.1582 = bf16[1,3111680]{1,0:T(2,128)(2,1)} reshape(bf16[3111680]{0:T(1024)(128)(2,1)} %get-tuple-element.133) | data formatting | bytes 12446720
  338.9 19.7 %slice_reduce_fusion.5 = bf16[524288]{0:T(1024)(128)(2,1)} fusion(bf16[1,3111680]{1,0:T(2,128)(2,1)} %reshape.1582), kind=kLoop, calls=%fused_computation.259 | loop fusion | bytes 2097152 | tf_op jit(solution)/shard_map/slice | solution.py:58
  358.6 46.8 %slice_reduce_fusion.2 = (bf16[1048576]{0:T(1024)(128)(2,1)}, bf16[1048576]{0:T(1024)(128)(2,1)S(1)}) fusion(bf16[1,3111680]{1,0:T(2,128)(2,1)} %reshape.1582), kind=kLoop, calls=%fused_computation.107 | loop fusion | bytes 8388608 | tf_op jit(solution)/shard_map/slice | solution.py:58
  405.4 60.8 %reshape.1584 = bf16[1,3111680]{1,0:T(2,128)(2,1)} reshape(bf16[3111680]{0:T(1024)(128)(2,1)} %get-tuple-element.134) | data formatting | bytes 12446720
  495.8 19.7 %slice_reduce_fusion.4 = bf16[524288]{0:T(1024)(128)(2,1)} fusion(bf16[1,3111680]{1,0:T(2,128)(2,1)} %reshape.1584), kind=kLoop, calls=%fused_computation.258 | loop fusion | bytes 2097152 | tf_op jit(solution)/shard_map/slice | solution.py:58
  515.5 47.4 %slice_reduce_fusion = (bf16[1048576]{0:T(1024)(128)(2,1)}, bf16[1048576]{0:T(1024)(128)(2,1)}) fusion(bf16[1,3111680]{1,0:T(2,128)(2,1)} %reshape.1584), kind=kLoop, calls=%fused_computation.105 | loop fusion | bytes 8388608 | tf_op jit(solution)/shard_map/slice | solution.py:58
  603.5 15.8 %add_multiply_fusion.1 = f32[1,5,96,960]{3,2,1,0:T(8,128)S(1)} fusion(bf16[1,5,96,960]{3,2,1,0:T(8,128)(2,1)S(1)} %fusion.258, f32[960]{0:T(1024)S(1)} %bitcast.857, f32[960]{0:T(1024)S(1)} %bitcast.697, f32[960]{0:T(1024)S(1)} %bitcast.699, f32[960]{0:T(1024)S(1)} %bitcast.701, f32[960]{0:T(1024)S(1)} %bitcast.703, f32[960]{0:T(1024)S(1)} %bitcast.705, ...), kind=kLoop, calls=%fused_computation.518 | loop fusion | flops 70963200 | bytes 42769920 | tf_op jit(solution)/shard_map/mul | solution.py:134
  666.6 15.9 %add_multiply_fusion = f32[1,5,96,960]{3,2,1,0:T(8,128)S(1)} fusion(bf16[1,5,96,960]{3,2,1,0:T(8,128)(2,1)S(1)} %fusion.257, f32[960]{0:T(1024)} %bitcast.856, f32[960]{0:T(1024)S(1)} %bitcast.795, f32[960]{0:T(1024)S(1)} %bitcast.797, f32[960]{0:T(1024)S(1)} %bitcast.799, f32[960]{0:T(1024)S(1)} %bitcast.801, f32[960]{0:T(1024)S(1)} %bitcast.803, ...), kind=kLoop, calls=%fused_computation.516 | loop fusion | flops 70963200 | bytes 42769920 | tf_op jit(solution)/shard_map/mul | solution.py:134
  793.9 16.2 %multiply_convert_fusion.3 = bf16[1,5,96,960]{3,2,1,0:T(8,128)(2,1)S(1)} fusion(bf16[1,5,96,960]{3,2,1,0:T(8,128)(2,1)S(1)} %get-tuple-element.164, bf16[1,3,96,960]{3,2,1,0:T(8,128)(2,1)} %collective-permute-done.4, bf16[1,3,96,960]{3,2,1,0:T(8,128)(2,1)} %collective-permute-done.5, bf16[1,11,102,960]{3,2,1,0:T(8,128)(2,1)S(1)} %select_maximum_fusion.2, ...), kind=kLoop, calls=%fused_computation.515 | loop fusion | flops 70963200 | bytes 41846400 | tf_op jit(solution)/shard_map/convert.301
  869.5 103.5 %concatenate.183 = bf16[3111680]{0:T(1024)(128)(2,1)} concatenate(bf16[512]{0:T(512)(128)(2,1)} %get-tuple-element.111, bf16[512]{0:T(512)(128)(2,1)} %get-tuple-element.129, bf16[524288]{0:T(1024)(128)(2,1)S(1)} %bitcast.619, bf16[1024]{0:T(1024)(128)(2,1)} %maximum_reduce_fusion.1, bf16[47040]{0:T(1024)(128)(2,1)S(1)} %copy-done.66, bf16[960]{0:T(1024)(128)(2,1)S(1)} %copy-done.258, ...), dimensions={0} | concatenate | bytes 12446720 | tf_op jit(solution)/shard_map/concatenate | solution.py:254
  973.0 14.0 convert_element_type.1400
  987.5 41.5 %reduce.112 = bf16[8,388960]{1,0:T(8,128)(2,1)} reduce(bf16[8,1,388960]{2,1,0:T(2,128)(2,1)} %convert_element_type.1400, bf16[]{:T(256)} %broadcast.887), dimensions={1}, to_apply=%convert_element_type.1400.reduce_sub_computation | reduce | bytes 12446722 | tf_op jit(solution)/shard_map/convert_element_type | solution.py:305
  1029.0 12.0 reshape.1657
  1051.4 16.0 %multiply_convert_fusion.2 = bf16[1,5,96,960]{3,2,1,0:T(8,128)(2,1)S(1)} fusion(bf16[1,5,96,960]{3,2,1,0:T(8,128)(2,1)S(1)} %get-tuple-element.152, bf16[1,3,96,960]{3,2,1,0:T(8,128)(2,1)} %collective-permute-done.6, bf16[1,3,96,960]{3,2,1,0:T(8,128)(2,1)S(1)} %copy-done.37, bf16[1,11,102,960]{3,2,1,0:T(8,128)(2,1)S(1)} %select_maximum_fusion, ...), kind=kLoop, calls=%fused_computation.514 | loop fusion | flops 70963200 | bytes 41846400 | tf_op jit(solution)/shard_map/convert.297
  1072.7 86.5 %concatenate.181 = bf16[3111680]{0:T(1024)(128)(2,1)} concatenate(bf16[512]{0:T(512)(128)(2,1)S(1)} %get-tuple-element.121, bf16[512]{0:T(512)(128)(2,1)S(1)} %get-tuple-element.125, bf16[524288]{0:T(1024)(128)(2,1)S(1)} %bitcast.620, bf16[1024]{0:T(1024)(128)(2,1)S(1)} %maximum_reduce_fusion, bf16[47040]{0:T(1024)(128)(2,1)S(1)} %reshape.1472, bf16[960]{0:T(1024)(128)(2,1)S(1)} %copy-done.259, ...), dimensions={0} | concatenate | bytes 12446720 | tf_op jit(solution)/shard_map/concatenate | solution.py:254
  1159.1 14.0 convert_element_type.1399
  1173.1 41.5 %reduce.113 = bf16[8,388960]{1,0:T(8,128)(2,1)} reduce(bf16[8,1,388960]{2,1,0:T(2,128)(2,1)} %convert_element_type.1399, bf16[]{:T(256)} %broadcast.887), dimensions={1}, to_apply=%convert_element_type.1399.reduce_sub_computation | reduce | bytes 12446722 | tf_op jit(solution)/shard_map/convert_element_type | solution.py:305
  1214.6 12.1 reshape.1659
  1231.6 16.2 %reshape.1658 = bf16[8,1,388960]{2,1,0:T(2,128)(2,1)} reshape(bf16[8,2,194480]{2,1,0:T(2,128)(2,1)} %all-to-all-done.1) | data formatting | bytes 12446720
  1247.8 104.8 %reduce_sum.1445 = bf16[388960]{0:T(1024)(128)(2,1)} reduce(bf16[8,1,388960]{2,1,0:T(2,128)(2,1)} %reshape.1658, bf16[]{:T(256)} %constant.23.clone.1), dimensions={0,1}, to_apply=%region_144.145 | reduce | flops 2722720 | bytes 7001282 | tf_op jit(solution)/shard_map/reduce_sum | solution.py:311
  1352.5 15.9 %reshape.1660 = bf16[8,1,388960]{2,1,0:T(2,128)(2,1)} reshape(bf16[8,2,194480]{2,1,0:T(2,128)(2,1)} %all-to-all-done) | data formatting | bytes 12446720
  1368.5 105.1 %reduce_sum.1381 = bf16[388960]{0:T(1024)(128)(2,1)} reduce(bf16[8,1,388960]{2,1,0:T(2,128)(2,1)} %reshape.1660, bf16[]{:T(256)} %constant.23.clone.1), dimensions={0,1}, to_apply=%region_79.80 | reduce | flops 2722720 | bytes 7001282 | tf_op jit(solution)/shard_map/reduce_sum | solution.py:311
  1476.1 65.9 %all-reduce.15.cloned.1.call-done = (bf16[388960]{0:T(1024)(128)(2,1)}, bf16[388960]{0:T(1024)(128)(2,1)}) async-done(((bf16[388960]{0:T(1024)(128)(2,1)}, bf16[388960]{0:T(1024)(128)(2,1)}), (bf16[388960]{0:T(1024)(128)(2,1)}, bf16[388960]{0:T(1024)(128)(2,1)})) %all-reduce.15.cloned.1.call-update) | async-done | bytes 1555856
  (912 shorter events, 349.8 us)
Async XLA Ops:
  7.2 250.0 %all-reduce.13.cloned.1.call-start = ((), (), s32[]{:S(2)}) async-start(), calls=%async_computation.2 | async-start | bytes 24895488
  25.8 542.8 %copy-start.234 = (f32[5,96]{1,0:T(8,128)}, f32[5,96]{1,0:T(8,128)S(1)}, u32[]{:S(2)}) copy-start(f32[5,96]{1,0:T(8,128)S(1)} %broadcast_multiply_fusion.11) | copy-start | bytes 5764
  26.3 542.4 %copy-start.251 = (f32[5,96]{1,0:T(8,128)}, f32[5,96]{1,0:T(8,128)S(1)}, u32[]{:S(2)}) copy-start(f32[5,96]{1,0:T(8,128)S(1)} %add_rsqrt_fusion.3) | copy-start | bytes 5764
  323.9 244.7 %copy-start.246 = (f32[1,512]{1,0:T(1,128)}, f32[1,512]{1,0:T(1,128)S(1)}, u32[]{:S(2)}) copy-start(f32[1,512]{1,0:T(1,128)S(1)} %get-tuple-element.190) | copy-start | bytes 6148
  480.5 122.5 %copy-start.72 = (f32[1,1,960]{2,1,0:T(1,128)}, f32[1,1,960]{2,1,0:T(1,128)S(1)}, u32[]{:S(2)}) copy-start(f32[1,1,960]{2,1,0:T(1,128)S(1)} %get-tuple-element.296) | copy-start | bytes 11524
  480.5 122.5 %copy-start.74 = (f32[1,1,960]{2,1,0:T(1,128)}, f32[1,1,960]{2,1,0:T(1,128)S(1)}, u32[]{:S(2)}) copy-start(f32[1,1,960]{2,1,0:T(1,128)S(1)} %get-tuple-element.297) | copy-start | bytes 11524
  480.5 122.5 %copy-start.76 = (f32[1,1,960]{2,1,0:T(1,128)}, f32[1,1,960]{2,1,0:T(1,128)S(1)}, u32[]{:S(2)}) copy-start(f32[1,1,960]{2,1,0:T(1,128)S(1)} %get-tuple-element.298) | copy-start | bytes 11524
  480.5 122.5 %copy-start.78 = (f32[1,1,960]{2,1,0:T(1,128)}, f32[1,1,960]{2,1,0:T(1,128)S(1)}, u32[]{:S(2)}) copy-start(f32[1,1,960]{2,1,0:T(1,128)S(1)} %get-tuple-element.299) | copy-start | bytes 11524
  480.5 122.5 %copy-start.80 = (f32[1,1,960]{2,1,0:T(1,128)}, f32[1,1,960]{2,1,0:T(1,128)S(1)}, u32[]{:S(2)}) copy-start(f32[1,1,960]{2,1,0:T(1,128)S(1)} %get-tuple-element.300) | copy-start | bytes 11524
  480.5 122.5 %copy-start.82 = (f32[1,1,960]{2,1,0:T(1,128)}, f32[1,1,960]{2,1,0:T(1,128)S(1)}, u32[]{:S(2)}) copy-start(f32[1,1,960]{2,1,0:T(1,128)S(1)} %get-tuple-element.301) | copy-start | bytes 11524
  480.5 122.5 %copy-start.84 = (f32[1,1,960]{2,1,0:T(1,128)}, f32[1,1,960]{2,1,0:T(1,128)S(1)}, u32[]{:S(2)}) copy-start(f32[1,1,960]{2,1,0:T(1,128)S(1)} %get-tuple-element.302) | copy-start | bytes 11524
  480.5 122.5 %copy-start.86 = (f32[1,1,960]{2,1,0:T(1,128)}, f32[1,1,960]{2,1,0:T(1,128)S(1)}, u32[]{:S(2)}) copy-start(f32[1,1,960]{2,1,0:T(1,128)S(1)} %get-tuple-element.303) | copy-start | bytes 11524
  480.5 122.5 %copy-start.88 = (f32[1,1,960]{2,1,0:T(1,128)}, f32[1,1,960]{2,1,0:T(1,128)S(1)}, u32[]{:S(2)}) copy-start(f32[1,1,960]{2,1,0:T(1,128)S(1)} %get-tuple-element.304) | copy-start | bytes 11524
  572.7 28.3 %collective-permute-start = (bf16[1,3,96,960]{3,2,1,0:T(8,128)(2,1)}, bf16[1,3,96,960]{3,2,1,0:T(8,128)(2,1)}, u32[]{:S(2)}, u32[]{:S(2)}) collective-permute-start(bf16[1,3,96,960]{3,2,1,0:T(8,128)(2,1)} %get-tuple-element.203), channel_id=1, source_target_pairs={{0,1},{1,2},{2,3},{4,5},{5,6},{6,7},{8,9},{9,10},{10,11},{12,13},{... | collective-permute-start | bytes 1658888 | tf_op jit(solution)/shard_map/ppermute | solution.py:18
  576.6 24.4 %collective-permute-start.1 = (bf16[1,3,96,960]{3,2,1,0:T(8,128)(2,1)}, bf16[1,3,96,960]{3,2,1,0:T(8,128)(2,1)}, u32[]{:S(2)}, u32[]{:S(2)}) collective-permute-start(bf16[1,3,96,960]{3,2,1,0:T(8,128)(2,1)} %get-tuple-element.204), channel_id=1, source_target_pairs={{1,0},{2,1},{3,2},{5,4},{6,5},{7,6},{9,8},{10,9},{11,10},{13,12},{... | collective-permute-start | bytes 1658888 | tf_op jit(solution)/shard_map/ppermute | solution.py:19
  645.0 16.1 %collective-permute-start.2 = (bf16[1,3,96,960]{3,2,1,0:T(8,128)(2,1)S(1)}, bf16[1,3,96,960]{3,2,1,0:T(8,128)(2,1)S(1)}, u32[]{:S(2)}, u32[]{:S(2)}) collective-permute-start(bf16[1,3,96,960]{3,2,1,0:T(8,128)(2,1)S(1)} %get-tuple-element.201), channel_id=1, source_target_pairs={{0,1},{1,2},{2,3},{4,5},{5,6},{6,7},{8,9},{9,10},{10,11},{12,13},{... | collective-permute-start | bytes 1658888 | tf_op jit(solution)/shard_map/ppermute | solution.py:18
  649.6 15.6 %collective-permute-start.3 = (bf16[1,3,96,960]{3,2,1,0:T(8,128)(2,1)S(1)}, bf16[1,3,96,960]{3,2,1,0:T(8,128)(2,1)S(1)}, u32[]{:S(2)}, u32[]{:S(2)}) collective-permute-start(bf16[1,3,96,960]{3,2,1,0:T(8,128)(2,1)S(1)} %get-tuple-element.202), channel_id=1, source_target_pairs={{1,0},{2,1},{3,2},{5,4},{6,5},{7,6},{9,8},{10,9},{11,10},{13,12},{... | collective-permute-start | bytes 1658888 | tf_op jit(solution)/shard_map/ppermute | solution.py:19
  771.5 20.0 %collective-permute-start.5 = (bf16[1,3,96,960]{3,2,1,0:T(8,128)(2,1)}, bf16[1,3,96,960]{3,2,1,0:T(8,128)(2,1)}, u32[]{:S(2)}, u32[]{:S(2)}) collective-permute-start(bf16[1,3,96,960]{3,2,1,0:T(8,128)(2,1)} %get-tuple-element.199), channel_id=1, source_target_pairs={{1,0},{2,1},{3,2},{5,4},{6,5},{7,6},{9,8},{10,9},{11,10},{13,12},{... | collective-permute-start | bytes 1658888 | tf_op jit(solution)/shard_map/ppermute | solution.py:19
  772.8 18.7 %collective-permute-start.4 = (bf16[1,3,96,960]{3,2,1,0:T(8,128)(2,1)}, bf16[1,3,96,960]{3,2,1,0:T(8,128)(2,1)}, u32[]{:S(2)}, u32[]{:S(2)}) collective-permute-start(bf16[1,3,96,960]{3,2,1,0:T(8,128)(2,1)} %get-tuple-element.200), channel_id=1, source_target_pairs={{0,1},{1,2},{2,3},{4,5},{5,6},{6,7},{8,9},{9,10},{10,11},{12,13},{... | collective-permute-start | bytes 1658888 | tf_op jit(solution)/shard_map/ppermute | solution.py:18
  862.8 185.3 %collective-permute-start.7 = (bf16[1,3,96,960]{3,2,1,0:T(8,128)(2,1)}, bf16[1,3,96,960]{3,2,1,0:T(8,128)(2,1)S(1)}, u32[]{:S(2)}, u32[]{:S(2)}) collective-permute-start(bf16[1,3,96,960]{3,2,1,0:T(8,128)(2,1)} %get-tuple-element.197), channel_id=1, source_target_pairs={{1,0},{2,1},{3,2},{5,4},{6,5},{7,6},{9,8},{10,9},{11,10},{13,12},{... | collective-permute-start | bytes 1658888 | tf_op jit(solution)/shard_map/ppermute | solution.py:19
  864.1 184.9 %collective-permute-start.6 = (bf16[1,3,96,960]{3,2,1,0:T(8,128)(2,1)}, bf16[1,3,96,960]{3,2,1,0:T(8,128)(2,1)}, u32[]{:S(2)}, u32[]{:S(2)}) collective-permute-start(bf16[1,3,96,960]{3,2,1,0:T(8,128)(2,1)} %get-tuple-element.198), channel_id=1, source_target_pairs={{0,1},{1,2},{2,3},{4,5},{5,6},{6,7},{8,9},{9,10},{10,11},{12,13},{... | collective-permute-start | bytes 1658888 | tf_op jit(solution)/shard_map/ppermute | solution.py:18
  1041.1 185.7 %all-to-all-start.1 = ((bf16[8,2,194480]{2,1,0:T(2,128)(2,1)}), bf16[8,2,194480]{2,1,0:T(2,128)(2,1)}, u32[]{:S(2)}, u32[]{:S(2)}) async-start(bf16[8,2,194480]{2,1,0:T(2,128)(2,1)} %reshape.1657), calls=%async_computation.1 | async-start | bytes 12451840 | tf_op jit(solution)/shard_map/all_to_all | solution.py:304
  1226.8 125.7 %all-to-all-start = ((bf16[8,2,194480]{2,1,0:T(2,128)(2,1)}), bf16[8,2,194480]{2,1,0:T(2,128)(2,1)}, u32[]{:S(2)}, u32[]{:S(2)}) async-start(bf16[8,2,194480]{2,1,0:T(2,128)(2,1)} %reshape.1659), calls=%async_computation | async-start | bytes 12451840 | tf_op jit(solution)/shard_map/all_to_all | solution.py:304
  1231.5 310.4 %all-reduce.15.cloned.1.call-start = ((), (), s32[]{:S(2)}) async-start(), calls=%async_computation.3 | async-start | bytes 3112960
  (278 other events, 2117.7 us)
Sparse Core Ops, SparseCore 0:
  24.4 232.7 all-reduce.12
  1473.7 68.1 all-reduce.14
where the time goes:
time: 1570 us; the launch traced here: 1550 us
  local copies, waits for them, and re-layouts  682 us (43%)
  other arithmetic  452 us (29%)
  waiting for transfers between devices  309 us (20%)
  matrix products  53.8 us (3%)
  starting transfers between devices  34.5 us (2%)
  between operations  21.2 us (1%)
    unnamed x4, waiting for transfers between devices  297 us
    unnamed x617, local copies, waits for them, and re-layouts  222 us
    reduce_sum x2, other arithmetic, body(): partial_sum = jnp.sum(received, 0)  210 us
    concatenate x2, local copies, waits for them, and re-layouts, layer_back(): return (grad_values, jnp.concatenate(flat_pieces))  190 us
    slice x14, local copies, waits for them, and re-layouts, unpack(): pieces[name] = flat[offset:offset + count].reshape(shape)  167 us
    convert_element_type x2, other arithmetic, body(): flat.reshape(image_count, -1).astype(jnp.bfloat16)  83 us
    another operation x112, local copies, waits for them, and re-layouts, layer_back(): kernel_rows.append(jnp.stack(kernel_cols))  35.7 us
    another operation x10, other arithmetic  34.8 us
  transfers between devices with their start and end apart: 12, of which 4 were waited for; matrix products, arithmetic and copies ran while one was open for 33% of the time, Pallas kernels for 0%

commit v1 on v0

v1 whole, which is shorter than its diff:
```python
import functools
import math
from types import SimpleNamespace

import jax
import jax.numpy as jnp
from jax import lax
from jax.experimental import pallas as pl
from jax.experimental.pallas import tpu as pltpu
from jax.sharding import PartitionSpec as P

BF = jnp.bfloat16
F32 = jnp.float32
THIRD = 1.0 / 3.0
LANES = 128
TILE = 16
UNIT = TILE * LANES
NT = (((1,), (1,)), ((), ()))
TN = (((0,), (0,)), ((), ()))
MESH = pl.DeviceIdType.MESH
LINK, HOP = 75e3, 3.2
LAST_LINK, LAST_HOP = 65e3, 4.0
VMEM_LIMIT = 62 * 1024 * 1024 + 512 * 1024
WIDTH = 512


def layout(width):
    first = width // 8
    mixed = 15 * width // 8
    return [
        ("norm_gain", (width,)),
        ("norm_shift", (width,)),
        ("inner_weight", (width, 2 * width)),
        ("inner_bias", (2 * width,)),
        ("kernel", (7, 7, mixed)),
        ("kernel_bias", (mixed,)),
        ("order_one", (first, 2 * first)),
        ("bias_one", (2 * first,)),
        ("order_two", (2 * first, 4 * first)),
        ("bias_two", (4 * first,)),
        ("order_three", (4 * first, 8 * first)),
        ("bias_three", (8 * first,)),
        ("outer_weight", (width, width)),
        ("outer_bias", (width,)),
        ("scale_mixer", (width,)),
        ("second_gain", (width,)),
        ("second_shift", (width,)),
        ("expand", (width, 4 * width)),
        ("expand_bias", (4 * width,)),
        ("reduce", (4 * width, width)),
        ("reduce_bias", (width,)),
        ("scale_mlp", (width,)),
    ]


def chunk_table():
    table, offset = {}, 0
    for name, shape in layout(WIDTH):
        table[name] = (offset // LANES, shape)
        offset += math.prod(shape)
    return table, offset


CHUNK, USED = chunk_table()
CHUNKS = USED // LANES
BODY_ROWS = -(-CHUNKS // 256) * 256
FLAT_ROWS = BODY_ROWS + 256
SPLIT = CHUNK["order_one"][0]
PART = -(-(SPLIT + 1) // TILE) * TILE
MIDDLE = BODY_ROWS - 16384
PLACE = {name: start for name, (start, _) in CHUNK.items()}
MOVED = {"expand_bias": (16080, 7904), "reduce_bias": (24288, 7936), "scale_mlp": (24288, 7936)}
for _name, (_from, _to) in MOVED.items():
    PLACE[_name] += _to - _from
KEPT_ROWS = 8192
TILES = [(row, row, 0, 16) for row in range(CHUNK["kernel"][0], PART, TILE)] + [
    (0, 0, 0, 8),
    (4096, 4096, 8, 16),
    (7904, 16080, 14, 16),
    (7920, 16096, 0, 14),
    (7936, 24288, 14, 16),
    (7952, 24304, 0, 6),
]
WIRED = ("reduce", "expand", "inner_weight")
GATES_END = CHUNK["expand"][0]
VECTORS = [
    name
    for name, shape in layout(WIDTH)
    if len(shape) == 1 and name != "kernel_bias"
]
MATRICES = [name for name, shape in layout(WIDTH) if len(shape) == 2]
PADDED = {name: CHUNK[name][1] for name in MATRICES}
PADDED["order_one"] = (LANES, LANES)


def lanes(index, size):
    return pl.ds(pl.multiple_of(index * size, size), size)


def loop(count, body):
    def step(index, carry):
        body(index)
        return carry

    lax.fori_loop(0, count, step, 0)


def column_sum(value):
    return jnp.sum(value.astype(F32), axis=0, keepdims=True)


def normal_of(values):
    mean = jnp.mean(values, -1, keepdims=True)
    centered = values - mean
    inverse = lax.rsqrt(jnp.mean(centered * centered, -1, keepdims=True) + 1e-06)
    return centered * inverse, inverse


def norm_back(grad_normed, normal, inverse, gain):
    scaled = grad_normed * gain
    return inverse * (
        scaled
        - jnp.mean(scaled, -1, keepdims=True)
        - normal * jnp.mean(scaled * normal, -1, keepdims=True)
    )


def product(left, right, dims=None):
    if dims is None:
        return jnp.dot(left, right, preferred_element_type=F32)
    return lax.dot_general(left, right, dims, preferred_element_type=F32)


def half_mask(rows):
    return lax.broadcasted_iota(jnp.int32, (rows, LANES), 1) < LANES // 2


def taps_from_flat(flat, taps, bias):
    low = half_mask(8)
    top = lax.broadcasted_iota(jnp.int32, (8, LANES), 0) == 0
    start = CHUNK["kernel"][0]

    def keep(tap, value):
        taps[8 * tap : 8 * tap + 8, :] = value

    for pair in range(25):
        base = start + 15 * pair
        even = pltpu.roll(flat[base : base + 8, :], LANES // 2, 1)
        down = pltpu.roll(even, 1, 0)
        keep(2 * pair, jnp.where(low, jnp.where(top, 0.0, down), even))
        odd = jnp.where(low & top, 0.0, flat[base + 7 : base + 15, :])
        if pair == 24:
            bias[...] = odd
        else:
            keep(2 * pair + 1, odd)


def taps_to_flat(taps, flat):
    low = half_mask(8)
    top = lax.broadcasted_iota(jnp.int32, (8, LANES), 0) == 0
    start = CHUNK["kernel"][0]
    for pair in range(25):
        base = start + 15 * pair
        even = pltpu.roll(taps[16 * pair : 16 * pair + 8, :], LANES // 2, 1)
        up = pltpu.roll(even, 7, 0)
        odd = taps[16 * pair + 8 : 16 * pair + 16, :]
        flat[base : base + 8, :] = jnp.where(low, even, up)
        last = pltpu.roll(even, 1, 0)
        flat[base + 7 : base + 15, :] = jnp.where(low & top, last, odd)


def weights_from_flat(flat, weights, vectors, taps, bias, beside):
    for name in MATRICES:
        start, (depth, width) = CHUNK[name]
        count = width // LANES
        block = min(depth, 256)
        target = getattr(weights, name)
        for tile in range(count):

            def move(index, tile=tile):
                row = pl.multiple_of(index * block, block)
                if count == 1:
                    source = pl.ds(start, block)
                else:
                    source = pl.ds(start + tile + row * count, block, stride=count)
                target[pl.ds(row, block), tile * LANES : (tile + 1) * LANES] = flat[
                    source, :
                ].astype(BF)

            if depth == block:
                move(0)
            else:
                loop(depth // block, move)
        beside.tick(depth * width * 1.6e-6)
    weights.order_one[LANES // 2 :, :] = jnp.zeros((LANES // 2, LANES), BF)
    for index, name in enumerate(VECTORS):
        start, (width,) = CHUNK[name]
        for tile in range(width // LANES):
            vectors[index : index + 1, tile * LANES : (tile + 1) * LANES] = flat[
                start + tile : start + tile + 1, :
            ]
    taps_from_flat(flat, taps, bias)


class Vectors:
    def __init__(self, ref):
        self.ref = ref

    def __getattr__(self, name):
        index = VECTORS.index(name)
        return self.ref[index : index + 1, : CHUNK[name][1][0]]

    def part(self, name, tile, size):
        index = VECTORS.index(name)
        return self.ref[index : index + 1, lanes(tile, size)]


def store_vector(flat, name, value, tile=0):
    count = value.shape[1] // LANES
    start = PLACE[name] + tile * count
    for index in range(count):
        flat[pl.ds(start + index, 1), :] = value[:, index * LANES : (index + 1) * LANES]


def store_matrix(r, name, value, row=0, tile=0):
    if name in r.wires:
        count = value.shape[1] // LANES
        for index in range(count):
            part = value[:, index * LANES : (index + 1) * LANES].astype(BF)
            r.wires[name][tile * count + index, pl.ds(row, value.shape[0]), :] = part
        return
    flat = r.flat
    start, (depth, width) = CHUNK[name]
    count = width // LANES
    rows = value.shape[0]
    for index in range(value.shape[1] // LANES):
        first = start + row * count + tile * (value.shape[1] // LANES) + index
        if count == 1:
            flat[pl.ds(first, rows), :] = value
        else:
            flat[pl.ds(first, rows, stride=count), :] = value[
                :, index * LANES : (index + 1) * LANES
            ]


class Grid:
    def __init__(self, rows, cols):
        self.rows, self.cols = rows, cols
        self.pixels = rows * cols
        self.tall, self.wide = rows + 6, cols + 6
        self.halo = 3 * cols
        self.all = self.tall * cols
        self.step = 12
        self.blocks = cols // self.step
        self.taps_step = 12
        self.taps_blocks = cols // (2 * self.taps_step)

    def at(self, row, place):
        return (row * self.wide + place) * 8


def register(ref, index):
    return ref[pl.ds(pl.multiple_of(index, 8), 8), :]


def tree(terms):
    while len(terms) > 1:
        left = terms[len(terms) // 2 * 2 :]
        terms = [a + b for a, b in zip(terms[::2], terms[1::2])] + left
    return terms[0]


def depthwise(grid, field, taps, target, flip, finish, beside):
    def block_at(row, block):
        base = grid.at(row, block * grid.step)
        sums = [None] * grid.step
        for i in range(7):
            line = [
                register(field, base + grid.at(i, q)) for q in range(grid.step + 6)
            ]
            for j in range(7):
                tap = 7 * i + j
                tap = 48 - tap if flip else tap
                weight = taps[tap * 8 : tap * 8 + 8, :]
                for c in range(grid.step):
                    term = line[c + j] * weight
                    sums[c] = term if sums[c] is None else sums[c] + term
        first = (row * grid.cols + block * grid.step) * 8
        for c in range(grid.step):
            target[pl.ds(pl.multiple_of(first + c * 8, 8), 8), :] = finish(sums[c])

    pairs = grid.blocks // 2

    def body(index):
        row, pair = index // pairs, index % pairs
        block_at(row, 2 * pair)
        block_at(row, 2 * pair + 1)
        beside.inside(index, grid.rows * pairs, 10, 12.0)

    loop(grid.rows * pairs, body)


def depthwise_taps(grid, field, grads, target, beside, first, last):
    step, blocks = grid.taps_step, grid.taps_blocks

    def per_row(i):
        def body(index, sums):
            row, block = index // blocks, index % blocks
            for part in range(2):
                col = (2 * block + part) * step
                start = grid.at(row + 3, col + 3)
                grad = [register(grads, start + 8 * c) for c in range(step)]
                base = grid.at(row + i, col)
                line = [register(field, base + 8 * q) for q in range(step + 6)]
                sums = tuple(
                    sums[j] + tree([line[c + j] * grad[c] for c in range(step)]) for j in range(7)
                )
            return sums

        zero = jnp.zeros((8, LANES), F32)
        sums = lax.fori_loop(0, grid.rows * blocks, body, (zero,) * 7)
        for j in range(7):
            target[pl.ds(pl.multiple_of((i * 7 + j) * 8, 8), 8), :] = sums[j]
        beside.inside(i - first, last - first, last - first, 1.7 * (last - first))

    loop(last - first, lambda index: per_row(index + first))


def to_field(grid, source, field, first, count):
    zero = jnp.zeros((24, LANES), F32)

    def per_row(row):
        rows = lanes(row, grid.cols)
        base = grid.at(first + row, 0)
        field[pl.ds(pl.multiple_of(base, 8), 24), :] = zero
        field[pl.ds(pl.multiple_of(base + (grid.cols + 3) * 8, 8), 24), :] = zero
        for tile in range(8):
            value = source[rows, tile * LANES : (tile + 1) * LANES].astype(F32)
            field[pl.ds(base + 24 + tile, grid.cols, stride=8), :] = value

    loop(count, per_row)


def gelu_parts(hidden):
    half = 0.5 * (1.0 + lax.erf(hidden * (1.0 / math.sqrt(2.0))))
    bell = jnp.exp(hidden * hidden * -0.5) * (1.0 / math.sqrt(2.0 * math.pi))
    return hidden * half, half + hidden * bell


LINE_AT = {1: (0, 128), 2: (128, 256), 3: (384, 512)}
GATE_AT = {0: (0, 128), 1: (128, 128), 2: (256, 256), 3: (512, 512)}
ORDER = {1: "order_one", 2: "order_two", 3: "order_three"}
SECOND = ("second_gain", "second_shift", "scale_mixer", "outer_bias")
ENDS = "ends"
CREDIT, SOURCE, BEFORE, DASH = "credit", "source_{}", "before_{}", "_"
SUMS, SENDS, RECEIVES = "sums_{}_{}_{}", "sends_{}_{}", "receives_{}_{}"
BIAS = {1: "bias_one", 2: "bias_two", 3: "bias_three"}


def mixed_tiles(grid, mixed, first, count):
    parts = [
        mixed[pl.ds(first + t, grid.pixels, stride=8), :] for t in range(count)
    ]
    return parts[0] if count == 1 else jnp.concatenate(parts, axis=1)


class Steps:
    def __init__(self, pace=(LINK, HOP)):
        self.waiting, self.clock, self.pace = [], 0.0, pace

    def add(self, steps):
        self.waiting += [(self.clock + time, step) for time, step in steps]
        self.waiting.sort(key=lambda item: item[0])

    def due(self, time):
        self.clock += time
        now = [step for ready, step in self.waiting if ready <= self.clock]
        self.waiting = self.waiting[len(now) :]
        return now

    def tick(self, time):
        for step in self.due(time):
            step()

    def inside(self, index, count, parts, time):
        period = count // parts
        places = [(part * period, self.due(time / parts)) for part in range(parts)]
        places = [(place, steps) for place, steps in places if steps]

        def run(steps):
            for step in steps:
                step()

        def some():
            for place, steps in places:
                pl.when(index == place)(functools.partial(run, steps))

        if places and period > 1:
            pl.when(index % period == 0)(some)
        elif places:
            some()

    def drain(self, between=lambda: None):
        ends = [step for _, step in self.waiting if hasattr(step, ENDS)]
        for _, step in self.waiting:
            if not hasattr(step, ENDS):
                step()
        for step in ends[:-2]:
            step()
        between()
        for step in ends[-2:]:
            step()
        self.waiting = []


def forward(grid, w, v, taps, r, beside, halo_here, written):
    own = (r.x, 3, grid.rows)
    parts = (own, (r.x_up, 0, 3), (r.x_down, 3 + grid.rows, 3))
    gain, shift = v.norm_gain, v.norm_shift
    for source, first, count in parts:

        def norm_row(index, source=source, first=first):
            rows = lanes(index, grid.cols)
            normal, _ = normal_of(source[rows, :].astype(F32))
            r.normed_all[lanes(index + first, grid.cols), :] = (
                normal * gain + shift
            ).astype(BF)

        loop(count, norm_row)
        if first == 3:
            halo_here()
        beside.tick(0.6)

    side = pl.ds(0, grid.halo)
    rest = {
        0: r.active.at[side, pl.ds(0, 2 * WIDTH)],
        3: r.gated,
        3 + grid.rows: r.active.at[side, pl.ds(2 * WIDTH, 2 * WIDTH)],
    }

    def inner_tile(tile):
        columns = lanes(tile, 256)
        weight = w.inner_weight[:, columns]
        bias = v.part("inner_bias", tile, 256)
        for _, first, count in parts:
            rows = slice(first * grid.cols, (first + count) * grid.cols)
            inner = product(r.normed_all[rows, :], weight) + bias
            if first == 3:

                @pl.when(tile == 0)
                def _():
                    r.head[...] = inner[:, :LANES]

            valid = r.mask[rows, :] > 0.0
            valid = jnp.concatenate([valid, valid], axis=1)
            rest[first][:, columns] = jnp.where(valid, inner, 0.0).astype(BF)
        beside.inside(tile, 4, 4, 2.0)

    loop(2 * WIDTH // 256, inner_tile)
    for _, first, count in parts:
        to_field(grid, rest[first], r.field, first, count)
        beside.tick(0.5)
    written()

    bias = r.bias[...]
    depthwise(
        grid, r.field, taps, r.mixed, False, lambda s: (s + bias) * THIRD, beside
    )

    low = half_mask(grid.pixels)
    first_gate = pltpu.roll(mixed_tiles(grid, r.mixed, 0, 1), LANES // 2, 1)
    gated = jnp.where(low, r.head[...] * first_gate, 0.0)
    r.gated[:, :LANES] = gated.astype(BF)
    for k in (1, 2, 3):
        at, size = GATE_AT[k - 1]
        low_gated = r.gated[:, at : at + size]
        at, size = LINE_AT[k]
        for tile in range(max(size // 256, 1)):
            part = min(size, 256)
            inside = slice(tile * part, (tile + 1) * part)
            line = product(low_gated, getattr(w, ORDER[k])[:, inside]) + getattr(v, BIAS[k])[:, inside]
            r.lines[:, at + tile * part : at + (tile + 1) * part] = line.astype(BF)
            start = GATE_AT[k][0] + tile * part
            gate = mixed_tiles(grid, r.mixed, start // LANES, part // LANES)
            r.gated[:, start : start + part] = (line * gate).astype(BF)
        beside.tick(0.7)

    def outer_tile(tile):
        columns = lanes(tile, 256)
        branch = product(r.gated[:, 512:], w.outer_weight[:, columns]) + v.part(
            "outer_bias", tile, 256
        )
        r.branch_a[:, columns] = branch.astype(BF)
        r.middle[:, columns] = (
            r.x[:, columns].astype(F32) + v.part("scale_mixer", tile, 256) * branch
        )

    loop(WIDTH // 256, outer_tile)
    beside.tick(0.7)
    gain, shift = v.second_gain, v.second_shift

    def second_norm(index):
        rows = lanes(index, grid.cols)
        normal, _ = normal_of(r.middle[rows, :])
        r.normed_b[rows, :] = (normal * gain + shift).astype(BF)

    loop(grid.rows, second_norm)
    beside.tick(0.6)
    written()

    def expand_tile(tile):
        columns = lanes(tile, 256)
        hidden = product(r.normed_b[...], w.expand[:, columns]) + v.part(
            "expand_bias", tile, 256
        )
        active, slope = gelu_parts(hidden)
        r.active[:, columns] = active.astype(BF)
        r.slope[:, columns] = slope.astype(BF)

    def expand_pair(index):
        expand_tile(2 * index)
        expand_tile(2 * index + 1)
        beside.inside(index, 4, 4, 5.0)

    loop(4, expand_pair)
    written()

    def reduce_tile(tile):
        columns = lanes(tile, 256)
        branch = product(r.active[...], w.reduce[:, columns]) + v.part(
            "reduce_bias", tile, 256
        )
        r.branch_b[:, columns] = branch.astype(BF)
        result = r.middle[:, columns] + v.part("scale_mlp", tile, 256) * branch
        r.result[:, columns] = result
        beside.inside(tile, 2, 2, 1.0)

    loop(WIDTH // 256, reduce_tile)
    written()


def backward_one(grid, w, v, r, flat, beside, needed, halfway, expanded, widest_here):
    def reduce_in(tile):
        columns = lanes(tile, 256)
        grad = r.grad[:, columns].astype(F32)
        store_vector(flat, "scale_mlp", column_sum(grad * r.branch_b[:, columns].astype(F32)), tile)
        low = (grad * v.part("scale_mlp", tile, 256)).astype(BF)
        r.low[:, columns] = low
        store_vector(flat, "reduce_bias", column_sum(low), tile)

    loop(WIDTH // 256, reduce_in)
    needed()
    r.turned[...] = r.normed_b[...].T
    beside.tick(1.0)

    def expand_tile(tile):
        columns = lanes(tile, 256)
        store_matrix(
            r, "reduce", product(r.active[:, columns], r.low[...], TN), row=tile * 256
        )
        active = product(r.low[...], w.reduce[columns, :], NT)
        hidden = (active * r.slope[:, columns].astype(F32)).astype(BF)
        r.slope[:, columns] = hidden
        store_vector(flat, "expand_bias", column_sum(hidden), tile)
        store_matrix(r, "expand", product(r.turned[...], hidden), tile=tile)

    def expand_pair(index, first):
        expand_tile(2 * index + first)
        expand_tile(2 * index + first + 1)
        beside.inside(index, 2, 2, 3.7)

    loop(2, lambda index: expand_pair(index, 0))
    halfway()
    loop(2, lambda index: expand_pair(index, 4))
    expanded()
    needed()

    def expand_in(tile):
        columns = lanes(tile, 256)
        r.wide[:, columns] = product(r.slope[...], w.expand[columns, :], NT)

    loop(WIDTH // 256, expand_in)
    beside.tick(1.2)
    gain, scale = v.second_gain, v.scale_mixer

    def second_back(index, sums):
        rows = lanes(index, grid.cols)
        normal, inverse = normal_of(r.middle[rows, :])
        grad = r.wide[rows, :]
        back = r.grad[rows, :].astype(F32) + norm_back(grad, normal, inverse, gain)
        branch = r.branch_a[rows, :].astype(F32)
        r.back[rows, :] = back
        low = (back * scale).astype(BF)
        r.low[rows, :] = low
        return (
            sums[0] + column_sum(grad * normal),
            sums[1] + column_sum(grad),
            sums[2] + column_sum(back * branch),
            sums[3] + column_sum(low),
        )

    zero = jnp.zeros((1, WIDTH), F32)
    sums = lax.fori_loop(0, grid.rows, second_back, (zero,) * 4)
    for name, value in zip(SECOND, sums):
        store_vector(flat, name, value)
    beside.tick(1.0)
    needed()

    r.turned[...] = r.gated[:, 512:].T

    def outer_tile(tile):
        columns = lanes(tile, 256)
        store_matrix(
            r, "outer_weight", product(r.turned[...], r.low[:, columns]), tile=tile
        )
        r.wide[:, columns] = product(r.low[...], w.outer_weight[columns, :], NT)

    loop(WIDTH // 256, outer_tile)
    beside.tick(1.2)

    for k in (3, 2, 1):
        at, size = LINE_AT[k]
        start = GATE_AT[k][0]
        part = min(size, 256)
        for tile in range(size // part):
            inside = slice(tile * part, (tile + 1) * part)
            grad = r.wide[:, inside]
            gate = mixed_tiles(grid, r.mixed, (start + tile * part) // LANES, part // LANES)
            low = (grad * gate).astype(BF)
            r.low[:, inside] = low
            store_vector(flat, BIAS[k], column_sum(low), tile)
            dm = grad * r.lines[:, at + tile * part : at + (tile + 1) * part].astype(F32)
            r.gated[:, start + tile * part : start + (tile + 1) * part] = (dm * THIRD).astype(BF)
        before, depth = GATE_AT[k - 1]
        grad = product(r.gated[:, before : before + depth], r.low[:, :size], TN)
        store_matrix(r, ORDER[k], grad[: CHUNK[ORDER[k]][1][0], :])
        r.wide[:, :depth] = product(r.low[:, :size], getattr(w, ORDER[k])[...], NT)
        if k == 3:
            widest_here()
        beside.tick(1.3)

    low = half_mask(grid.pixels)
    grad = r.wide[:, :LANES]
    first_gate = pltpu.roll(mixed_tiles(grid, r.mixed, 0, 1), LANES // 2, 1)
    dm = pltpu.roll(grad * r.head[...], LANES // 2, 1)
    r.head[...] = grad * first_gate
    r.gated[:, :LANES] = jnp.where(low, 0.0, dm * THIRD).astype(BF)


def backward_two(grid, w, v, taps, r, flat, beside, needed, halo_here, inner_here, before):
    needed()
    to_field(grid, r.gated, r.grads, 3, grid.rows)
    beside.tick(0.8)
    depthwise_taps(grid, r.field, r.grads, r.taps_grad, beside, 0, before)
    halo_here()
    to_field(grid, r.grad_up, r.grads, 0, 3)
    to_field(grid, r.grad_down, r.grads, 3 + grid.rows, 3)
    beside.tick(1.5)
    depthwise(grid, r.grads, taps, r.mixed, True, lambda s: s, beside)
    low = half_mask(grid.cols)
    for row in range(grid.rows):
        rows = slice(row * grid.cols, (row + 1) * grid.cols)
        valid = r.mask_own[rows, :] > 0.0
        for tile in range(8):
            value = r.mixed[pl.ds(row * grid.cols * 8 + tile, grid.cols, stride=8), :]
            value = jnp.where(valid, value, 0.0)
            if tile == 0:
                value = jnp.where(low, r.head[rows, :], value)
            r.active[rows, tile * LANES : (tile + 1) * LANES] = value.astype(BF)
    beside.tick(0.8)

    r.turned[...] = r.normed[...].T

    def inner_tile(tile):
        columns = lanes(tile, 256)
        grad = r.active[:, columns]
        store_vector(flat, "inner_bias", column_sum(grad), tile)
        store_matrix(r, "inner_weight", product(r.turned[...], grad), tile=tile)
        beside.inside(tile, 4, 4, 2.5)

    loop(2 * WIDTH // 256, inner_tile)
    inner_here()
    if before < 7:
        depthwise_taps(grid, r.field, r.grads, r.taps_grad, beside, before, 7)
    for tile in range(8):
        value = r.gated[:, tile * LANES : (tile + 1) * LANES]
        r.taps_grad[49 * 8 + tile : 49 * 8 + tile + 1, :] = column_sum(value)
    taps_to_flat(r.taps_grad, flat)

    def first_tile(tile):
        columns = lanes(tile, 256)
        r.wide[:, columns] = product(r.active[:, : 2 * WIDTH], w.inner_weight[columns, :], NT)

    loop(WIDTH // 256, first_tile)
    beside.tick(0.8)
    gain = v.norm_gain

    def first_back(index, sums):
        rows = lanes(index, grid.cols)
        normal, inverse = normal_of(r.x[rows, :].astype(F32))
        grad = r.wide[rows, :]
        result = r.back[rows, :] + norm_back(grad, normal, inverse, gain)
        r.input_grad[rows, :] = result.astype(r.input_grad.dtype)
        return (sums[0] + column_sum(grad * normal), sums[1] + column_sum(grad))

    zero = jnp.zeros((1, WIDTH), F32)
    sums = lax.fori_loop(0, grid.rows, first_back, (zero,) * 2)
    store_vector(flat, "norm_gain", sums[0])
    store_vector(flat, "norm_shift", sums[1])


def narrow(flat, low, first, last, base):
    block = 256

    def part(index, size):
        at = first + index * block
        source = pl.ds(pl.multiple_of(at, TILE), size)
        low[pl.ds(pl.multiple_of(at - base, TILE), size), :] = flat[source, :].astype(BF)

    loop((last - first) // block, lambda index: part(index, block))
    if (last - first) % block:
        part((last - first) // block, (last - first) % block)


def flat_from_slots(count, shard, small, slots, flat, widened=False):
    size = shard // UNIT * TILE

    def tile_of(index):
        return index * shard // UNIT * TILE

    def slot(index, row, rows):
        at = pl.ds(pl.multiple_of(index * small + row, TILE), rows)
        return slots[at, :].astype(F32)

    def widen(index):
        at = pl.ds(pl.multiple_of(tile_of(index) + TILE, TILE), size)
        flat[at, :] = slot(index, TILE, size)

    if not widened:
        return widen
    flat[0:TILE, :] = slot(0, 0, TILE)

    def edge(index):
        place = tile_of(index + 1)
        tail = slot(index, place - tile_of(index), TILE)
        flat[pl.ds(pl.multiple_of(place, TILE), TILE), :] = tail + slot(index + 1, 0, TILE)

    loop(count - 1, edge)
    last = tile_of(count)
    flat[last : last + TILE, :] = slot(count - 1, last - tile_of(count - 1), TILE)


def divide(value, by):
    return lax.div(value, lax.full_like(value, by))


def rest_of(value, by):
    return lax.rem(value, lax.full_like(value, by))


class Ring:
    def __init__(self, images, rows):
        self.side = side = math.isqrt(images // 2)
        assert 2 * side * side == images
        self.images, self.rows = images, rows
        self.img = lax.axis_index("img")
        self.row = lax.axis_index("row")
        self.core = rest_of(self.img, 2)
        place = divide(self.img, 2)
        a, b = divide(place, side), rest_of(place, side)
        one = self.core == 1
        self.u = jnp.where(one, a, b)
        self.w = jnp.where(one, b, a)
        self.us = [rest_of(self.u + o, side) for o in range(side)]
        self.ws = [rest_of(self.w + o, side) for o in range(side)]
        first_step = jnp.where(one, 2 * side, 2)
        second_step = jnp.where(one, 2, 2 * side)
        self.images_at = {
            (i, j): u * first_step + w * second_step + self.core
            for i, u in enumerate(self.us)
            for j, w in enumerate(self.ws)
        }
        self.row_at = [rest_of(self.row + o, rows) for o in range(rows)]
        self.near = [self.nearest(k) for k in range(rows)]
        self.other = self.img + 1 - 2 * self.core

    def image(self, i, j):
        return self.images_at[i % self.side, j % self.side]

    def along_row(self, o):
        return (self.img, self.row_at[o % self.rows])

    def nearest(self, k):
        if k == 0:
            return self.row
        row, last = self.row, self.rows - 1
        inside = row - (k + 1) // 2 if k % 2 else row + k // 2
        outside = jnp.where(row < last - row, k, last - k)
        return jnp.where(k <= 2 * jnp.minimum(row, last - row), inside, outside)

    def rank(self, row, other):
        last = self.rows - 1
        inside = jnp.where(other < row, 2 * (row - other) - 1, 2 * (other - row))
        outside = jnp.where(row < last - row, other, last - other)
        apart = jnp.maximum(row - other, other - row)
        return jnp.where(apart <= jnp.minimum(row, last - row), inside, outside)

    def along_first(self, o):
        return (self.image(o, 0), self.row)

    def along_second(self, o):
        return (self.image(0, o), self.row)

    def sibling(self):
        return (self.other, self.row)

    def partners(self):
        out = [self.along_row(o) for o in range(1, self.rows)]
        out += [self.along_first(o) for o in range(1, self.side)]
        out += [self.along_second(o) for o in range(1, self.side)]
        return out + [self.sibling()]

    def signal(self, semaphore):
        for partner in self.partners():
            pl.semaphore_signal(semaphore, inc=1, device_id=partner, device_id_type=MESH)

    def wait(self, semaphore):
        pl.semaphore_wait(semaphore, self.rows - 1 + 2 * (self.side - 1) + 1)


class Transfer:
    def __init__(self, ring, send, recv):
        self.ring, self.send, self.recv = ring, send, recv
        self.started = []

    def start(self, index, source, target, device, recv=None, when=None):
        def make():
            return pltpu.make_async_remote_copy(
                src_ref=source(),
                dst_ref=target(),
                send_sem=self.send.at[index],
                recv_sem=self.recv.at[index if recv is None else recv],
                device_id=device,
                device_id_type=MESH,
            )

        def run(act):
            if when is None:
                act()
            else:
                pl.when(when)(act)

        run(lambda: make().start())
        self.started.append(lambda: run(lambda: make().wait_send()))

    def arrived(self, index, target):
        pltpu.make_async_remote_copy(
            src_ref=target,
            dst_ref=target,
            send_sem=self.send.at[index],
            recv_sem=self.recv.at[index],
            device_id=self.ring.sibling(),
            device_id_type=MESH,
        ).wait_recv()

    def sent(self):
        for wait in self.started:
            wait()
        self.started = []


def gather_count(images, rows):
    side = math.isqrt(images // 2)
    return rows + 1 + rows * (side - 1) * (1 + side) + rows * side * side


class Gather(Transfer):
    def __init__(self, ring, own, slots, small, send, recv, local, single=False):
        super().__init__(ring, send, recv)
        self.single = single
        self.own, self.slots, self.small, self.local = own, slots, small, local
        rows, side = ring.rows, ring.side
        self.first_at = rows + 1
        self.second_at = self.first_at + (side - 1) * rows
        self.near_at = self.second_at + (side - 1) * side * rows
        images = {(q, o2): ring.image(-q, -o2) for q in range(side) for o2 in range(side)}
        self.blocks = {at: image * (rows * small) for at, image in images.items()}
        self.places = {
            (*at, k): block + ring.near[k] * small
            for at, block in self.blocks.items()
            for k in range(rows)
        }
        self.ranks = [ring.rank(ring.near[k], ring.row) - 1 for k in range(rows)]

    def block(self, q, o2):
        size = self.ring.rows * self.small
        return self.slots.at[pl.ds(pl.multiple_of(self.blocks[q, o2], TILE), size), :]

    def here(self, q, o2, k):
        start = pl.multiple_of(self.places[q, o2, k], TILE)
        return self.slots.at[pl.ds(start, self.small), :]

    def pass_on(self, source, q, o2, k):
        ring = self.ring
        rows, side = ring.rows, ring.side

        def target():
            return self.here(q, o2, k)

        if q == 0 and o2 == 0:
            for o in range(1, side):
                self.start(
                    self.first_at + (o - 1) * rows + k,
                    source,
                    target,
                    ring.along_first(o),
                )
        if o2 == 0:
            for o in range(1, side):
                self.start(
                    self.second_at + ((o - 1) * side + q) * rows + k,
                    source,
                    target,
                    ring.along_second(o),
                )
        if self.single:
            near = self.near_at + (o2 * side + q) * rows + k
            self.start(near, source, target, ring.sibling())
        elif k == rows - 1:
            if q == 0 and o2 == 0:
                pltpu.make_async_copy(self.own, self.here(0, 0, 0), self.local).wait()
            block = functools.partial(self.block, q, o2)
            self.start(self.near_at + o2 * side + q, block, block, ring.sibling())

    def begin(self):
        ring = self.ring

        def own():
            return self.own

        for k in range(1, ring.rows):
            self.start(
                k - 1,
                own,
                lambda: self.here(0, 0, 0),
                (ring.img, ring.near[k]),
                recv=self.ranks[k],
            )
        self.pass_on(own, 0, 0, 0)
        pltpu.make_async_copy(self.own, self.here(0, 0, 0), self.local).start()

    def arrivals(self):
        rows, side = self.ring.rows, self.ring.side
        arrivals = []
        for k in range(rows):
            if k:
                arrivals.append((k, 0, k - 1, (0, 0, k)))
            for o in range(1, side):
                arrivals.append((k + 1, 1, self.first_at + (o - 1) * rows + k, (o, 0, k)))
                for q in range(side):
                    index = self.second_at + ((o - 1) * side + q) * rows + k
                    arrivals.append((k + 1 + (q > 0), 2, index, (q, o, k)))
        arrivals.sort(key=lambda item: item[:2])
        return [(index, place) for _, _, index, place in arrivals]

    def step(self, index, place):
        self.arrived(index, self.here(*place))
        self.pass_on(lambda: self.here(*place), *place)

    def steps(self):
        arrivals = self.arrivals()
        first, per = 5.5, 25.0 / len(arrivals)
        return [
            (first + per * n, functools.partial(self.step, index, place))
            for n, (index, place) in enumerate(arrivals)
        ]

    def finish(self):
        ring = self.ring
        for index in range(self.near_at, self.near_at + ring.side * ring.side):
            self.arrived(index, self.block(0, 0))
        self.sent()

    def all_single(self, here):
        ring = self.ring
        steps = self.arrivals()
        for index, (q, o2, k) in steps:
            self.step(index, (q, o2, k))
            here(ring.image(-q, -o2), ring.near[k])
        pltpu.make_async_copy(self.own, self.here(0, 0, 0), self.local).wait()
        here(ring.img, ring.row)
        yield
        order = sorted(
            ((o2, q, k) for o2 in range(ring.side) for q in range(ring.side) for k in range(ring.rows)),
            key=lambda at: at[2] + (at[0] > 0) + (at[1] > 0),
        )
        for o2, q, k in order:
            self.arrived(self.near_at + (o2 * ring.side + q) * ring.rows + k, self.here(0, 0, 0))
            here(ring.image(-o2, -q) + 1 - 2 * ring.core, ring.near[k])
        self.sent()


def add_rows(count, size, target, sources):
    def part(at):
        total = None
        for source in sources:
            value = source(at).astype(F32)
            total = value if total is None else total + value
        target(at, total)

    block = max(TILE, min(LANES, 256 // count))
    loop(size // block, lambda index: part(pl.ds(pl.multiple_of(index * block, TILE), block)))
    if size % block:
        part(pl.ds(size // block * block, size % block))


def shifted(at, start):
    return pl.ds(pl.multiple_of(at.start + start, TILE), at.size)


class Sums(Transfer):
    def __init__(self, ring, source, span, shard, buffers, turn, send, recv, base=0):
        super().__init__(ring, send, recv)
        self.source, self.span, self.shard, self.base = source, span, shard, base
        self.lo, self.hi, self.count, self.size = span.lo, span.hi, span.count, span.size
        self.near, self.one, self.two, self.last, self.own, self.inbox = buffers
        self.turn, self.flat_size = turn, span.count * span.size
        self.line = ring.rows * self.size
        self.plane = ring.side * self.line
        self.half = ring.side * self.plane
        self.first_at = ring.side
        self.last_at = self.first_at + ring.side - 1
        self.owner_at = self.last_at + ring.rows - 1
        self.slots = self.inbox.shape[0]
        self.me = ((ring.core * ring.side + ring.w) * ring.side + ring.u) * ring.rows + ring.row
        self.device = ring.img * ring.rows + ring.row
        self.devices = ring.images * ring.rows
        self.mine = base + ring.core * self.half
        self.theirs = base + (1 - ring.core) * self.half
        self.planes = [w * self.plane for w in ring.ws]
        self.lines = [u * self.line for u in ring.us]
        self.places = [
            self.planes[0] + self.lines[0] + row * self.size for row in ring.row_at
        ]
        self.targets = [
            (divide(owner, ring.rows), rest_of(owner, ring.rows), here, self.slot(owner))
            for owner, here in self.owners()
        ]
        self.receives = [self.owner_at + slot for _, _, _, slot in self.targets]
        self.low, self.high = self.range_of(self.device)

    @staticmethod
    def scratch(images, rows, shard, span):
        side, n, size = math.isqrt(images // 2), span.count, span.size
        slots = Sums.slots_of(shard, span)
        return (
            ((n, side * side * rows * size, LANES), BF),
            ((side - 1, n, side * rows * size, LANES), BF),
            ((side - 1, n, rows * size, LANES), BF),
            ((rows - 1, n, size, LANES), BF),
            ((n * size, LANES), BF),
            ((slots, n * size, LANES), BF),
        )

    @staticmethod
    def slots_of(shard, span):
        if span.tiles:
            return len(span.tiles)
        return -(-(shard // LANES + 2) // (span.count * span.size)) + 1

    @staticmethod
    def number(images, rows, shard, span):
        side = math.isqrt(images // 2)
        return 1 + 2 * (side - 1) + rows - 1 + Sums.slots_of(shard, span) + 2

    def cut(self, ref, start, size):
        return ref.at[:, pl.ds(pl.multiple_of(start, TILE), size), :]

    def add(self, start, size, others):
        base = self.mine + start

        def keep(at, total):
            self.near[:, shifted(at, start), :] = total.astype(BF)

        terms = [
            lambda at: self.source[:, shifted(at, base), :],
            lambda at: self.near[:, shifted(at, start), :],
        ]
        add_rows(self.count, size, keep, terms + others)

    def begin(self):
        self.start(
            0,
            lambda: self.cut(self.source, self.theirs, self.half),
            lambda: self.near,
            self.ring.sibling(),
        )

    def second(self):
        ring = self.ring
        self.arrived(0, self.near)
        for j in range(1, ring.side):
            self.add(self.planes[j], self.plane, [])
            self.start(
                j,
                lambda j=j: self.cut(self.near, self.planes[j], self.plane),
                lambda j=j: self.one.at[j - 1],
                ring.along_second(j),
            )

    def across(self, place):
        return [
            lambda at, j=j: self.one[j - 1, :, shifted(at, place), :]
            for j in range(1, self.ring.side)
        ]

    def first(self):
        ring = self.ring
        for j in range(1, ring.side):
            self.arrived(j, self.one.at[j - 1])
        for i in range(1, ring.side):
            start = self.planes[0] + self.lines[i]
            self.add(start, self.line, self.across(self.lines[i]))
            self.start(
                self.first_at + i - 1,
                lambda i=i: self.cut(self.near, self.planes[0] + self.lines[i], self.line),
                lambda i=i: self.two.at[i - 1],
                ring.along_first(i),
            )

    def row(self):
        ring = self.ring
        terms = self.across(self.lines[0])
        for i in range(1, ring.side):
            self.arrived(self.first_at + i - 1, self.two.at[i - 1])
            terms.append(lambda at, i=i: self.two[i - 1, :, at, :])
        self.add(self.planes[0] + self.lines[0], self.line, terms)
        for o in range(1, ring.rows):
            self.start(
                self.last_at + o - 1,
                lambda o=o: self.cut(self.near, self.places[o], self.size),
                lambda o=o: self.last.at[o - 1],
                ring.along_row(o),
            )

    def row_of(self, piece):
        if self.span.tiles:
            plain = len(self.span.tiles) - 6
            valid = jnp.where(piece < plain, TILE, 0)
            out = (self.span.tiles[0][1] + piece * TILE, 0, valid)
            for index, (_, row, first, end) in list(enumerate(self.span.tiles))[plain:]:
                out = tuple(
                    jnp.where(piece == index, new, old) for new, old in zip((row, first, end), out)
                )
            return out
        row = self.lo + piece * self.flat_size
        return row, 0, jnp.minimum(self.hi - row, self.flat_size)

    def range_of(self, owner):
        first = divide(owner * self.shard, LANES) - self.lo
        last = divide((owner + 1) * self.shard - 1, LANES)
        last = jnp.minimum(last, self.hi - 1) - self.lo
        low = divide(jnp.maximum(first, 0), self.flat_size)
        high = divide(jnp.maximum(last + self.flat_size, 0), self.flat_size) - 1
        return low, jnp.minimum(high, self.devices - 1)

    def slot(self, owner):
        return self.me if self.span.tiles else jnp.maximum(self.me - self.range_of(owner)[0], 0)

    def owners(self):
        row, begin, end = self.row_of(self.me)
        there = end > begin
        first = jnp.minimum(divide((row + begin) * LANES, self.shard), self.devices - 1)
        last = divide(jnp.maximum((row + end) * LANES - 1, 0), self.shard)
        last = jnp.minimum(last, self.devices - 1)
        return (
            (first, there & (first != self.device)),
            (last, there & (last > first) & (last != self.device)),
        )

    def final(self):
        ring = self.ring
        terms = [lambda at: self.near[:, shifted(at, self.places[0]), :]]
        for o in range(1, ring.rows):
            self.arrived(self.last_at + o - 1, self.last.at[o - 1])
            terms.append(lambda at, o=o: self.last[o - 1, :, at, :])

        def keep(at, total):
            if self.count == 1:
                self.turn[at, :] = total[0]
                return
            for tile in range(self.count):
                first = at.start * self.count + tile
                self.turn[pl.ds(first, at.size, stride=self.count), :] = total[tile]

        add_rows(self.count, self.size, keep, terms)
        self.own[...] = self.turn[: self.flat_size, :].astype(BF)
        for t, (image, row, here, slot) in enumerate(self.targets):
            self.start(
                self.owner_at + self.slots + t,
                lambda: self.own,
                lambda slot=slot: self.inbox.at[slot],
                (image, row),
                recv=self.receives[t],
                when=here,
            )

    def collect(self, target, margin):
        low, high = self.low, self.high
        for t in range(self.slots):
            if self.span.tiles:
                _, row, begin, end = self.span.tiles[t]
                first = (row + begin) * LANES // self.shard
                last = ((row + end) * LANES - 1) // self.shard
                here, piece = (self.device >= first) & (self.device <= last), t
            else:
                here, piece = low + t <= high, low + t
                row, begin, end = self.row_of(piece)

            @pl.when(here)
            def _(t=t, piece=piece, row=row, begin=begin, end=end):
                mine = piece == self.me

                @pl.when(mine)
                def _():
                    self.inbox[t] = self.own[...]

                @pl.when(jnp.logical_not(mine))
                def _():
                    self.arrived(self.owner_at + t, self.inbox.at[t])

                start = row - divide(self.device * self.shard, UNIT) * TILE + margin
                if not self.span.tiles and self.lo % 8 == 0 and self.flat_size % 8 == 0:
                    start = pl.multiple_of(start, 8)
                if self.span.tiles:
                    start = pl.multiple_of(start, TILE)
                at = pl.ds(start, self.flat_size)
                index = lax.broadcasted_iota(jnp.int32, (self.flat_size, LANES), 0)
                target[at, :] = jnp.where(
                    (index >= begin) & (index < end), self.inbox[t].astype(F32), target[at, :]
                )

    def steps(self, target, margin, pace, delay=0.0, halo=0.0):
        unit = self.flat_size * LANES * 2 / pace[0]
        hop, out, time = pace[1], [], 0.0
        for step, after in (
            (self.begin, 16 * unit / 6),
            (self.second, 8 * unit),
            (self.first, 4 * unit),
            (self.row, 8 * unit),
            (self.final, 3 * unit + 2.0),
        ):
            if step == self.row:
                time = max(time, halo)
            out.append((time, step))
            time += after + hop
            if step == self.begin:
                time += delay

        def collect():
            self.collect(target, margin)

        collect.ends = True
        return out + [(time + 2 * hop, collect)]


class Halo(Transfer):
    def __init__(self, ring, grid, source, above, below, send, recv, first=0, width=None):
        super().__init__(ring, send, recv)
        columns = pl.ds(first, source.shape[1] if width is None else width)
        above, below = above.at[:, columns], below.at[:, columns]
        self.has_above, self.has_below = ring.row > 0, ring.row < ring.rows - 1
        self.above, self.below = above, below
        halo, pixels = grid.halo, grid.pixels
        self.moves = (
            (0, source.at[pl.ds(pixels - halo, halo), columns], above, 1, self.has_below, self.has_above),
            (1, source.at[pl.ds(0, halo), columns], below, ring.rows - 1, self.has_above, self.has_below),
        )

    def make(self, index, source, target, o):
        return pltpu.make_async_remote_copy(
            src_ref=source,
            dst_ref=target,
            send_sem=self.send.at[index],
            recv_sem=self.recv.at[index],
            device_id=self.ring.along_row(o),
            device_id_type=MESH,
        )

    def begin(self):
        for index, source, target, o, sends, gets in self.moves:

            @pl.when(sends)
            def _():
                self.make(index, source, target, o).start()

            @pl.when(jnp.logical_not(gets))
            def _():
                target[...] = jnp.zeros(target.shape, target.dtype)

    def finish(self):
        for index, source, target, o, sends, gets in self.moves:

            @pl.when(gets)
            def _():
                self.make(index, source, target, o).wait_recv()

            @pl.when(sends)
            def _():
                self.make(index, source, target, o).wait_send()


def call(kernel, identity, ins, outs, scratch, sems, limits, fetched=(), spilled=(), placed=None):
    placed = placed or {}
    fetch = {k: v for group in fetched for k, v in group.items()}
    spill = {k: v for group in spilled for k, v in group.items()}
    names = list(ins) + list(limits) + list(fetch) + list(outs) + list(spill) + list(placed)
    direct = set(ins) | set(limits) | set(outs) | set(placed)
    buffers = {k: (v.shape, v.dtype) for k, v in fetch.items()}
    buffers.update({k: v for k, v in spill.items() if k not in scratch})
    buffers.update(scratch)
    counts = dict(sems, fetch_sem=max(len(fetch), 1), spill_sem=max(len(spill), 1))

    def run(*refs):
        given = dict(zip(names, refs))
        rest = dict(zip(list(buffers) + list(counts) + [CREDIT], refs[len(names) :]))
        r = SimpleNamespace(**{k: v for k, v in given.items() if k in direct})
        for k, v in rest.items():
            setattr(r, k, v)
        groups = [list(group) for group in fetched]
        copies = {
            k: pltpu.make_async_copy(given[k], rest[k], r.fetch_sem.at[i])
            for i, k in enumerate(fetch)
        }
        for copy in copies.values():
            copy.start()

        def needed():
            if groups:
                for k in groups.pop(0):
                    copies[k].wait()

        leaving = [list(group) for group in spilled]
        gone, started = [], []

        def written():
            if leaving:
                for k in leaving.pop(0):
                    copy = pltpu.make_async_copy(
                        getattr(r, k), given[k], r.spill_sem.at[len(started)]
                    )
                    started.append(k)
                    copy.start()
                    gone.append(copy)

        def settled():
            while gone:
                gone.pop().wait()

        r.needed, r.written, r.settled = needed, written, settled
        kernel(r)
        while leaving:
            written()
        while groups:
            needed()
        settled()

    vmem = pl.BlockSpec(memory_space=pltpu.VMEM)
    smem = pl.BlockSpec(memory_space=pltpu.SMEM)
    anywhere = pl.BlockSpec(memory_space=pl.ANY)
    shapes = list(outs.values()) + list(spill.values()) + list(placed.values())
    results = pl.pallas_call(
        run,
        out_shape=[jax.ShapeDtypeStruct(*shape) for shape in shapes],
        in_specs=[vmem] * len(ins) + [smem] * len(limits) + [anywhere] * len(fetch),
        out_specs=[vmem] * len(outs) + [anywhere] * (len(spill) + len(placed)),
        scratch_shapes=[pltpu.VMEM(*shape) for shape in buffers.values()]
        + [
            pltpu.SemaphoreType.DMA(count if isinstance(count, tuple) else (count,))
            for count in counts.values()
        ]
        + [pltpu.SemaphoreType.REGULAR],
        compiler_params=pltpu.CompilerParams(
            collective_id=identity, has_side_effects=True, vmem_limit_bytes=VMEM_LIMIT
        ),
    )(*ins.values(), *limits.values(), *fetch.values())
    return SimpleNamespace(**dict(zip(names[len(ins) + len(limits) + len(fetch) :], results)))


def fill_mask(grid, row, heights, widths, mask, first, count):
    col = lax.broadcasted_iota(jnp.int32, (grid.cols, LANES), 0)
    for index in range(count):
        line = jnp.full((grid.cols, LANES), row * grid.rows + first + index, jnp.int32)
        valid = (line >= 0) & (line < heights[0]) & (col < widths[0])
        mask[index * grid.cols : (index + 1) * grid.cols, :] = jnp.where(valid, 1.0, 0.0)


def align_in(start, small, raw, own, flat, layer):
    shift, down = start % LANES, start // LANES % TILE
    low = lax.broadcasted_iota(jnp.int32, (small, LANES), 1) < shift
    count, second = raw.shape[1], 2048
    flat[0:8, :] = jnp.zeros((8, LANES), F32)
    flat[8 : 8 + count, :] = raw[layer].astype(F32)
    flat[8 + count : 40 + count, :] = jnp.zeros((32, LANES), F32)
    before = pltpu.roll(flat[7 : 7 + small, :], shift, 1)
    here = pltpu.roll(flat[8 : 8 + small, :], shift, 1)
    flat[second : second + TILE, :] = jnp.zeros((TILE, LANES), F32)
    flat[pl.ds(second + down, small), :] = jnp.where(low, before, here)
    own[layer] = flat[second : second + small, :].astype(BF)


def align_out(start, margin, summed, result, layer):
    shift, down = start % LANES, start // LANES % TILE + margin
    count = result.shape[1]
    low = lax.broadcasted_iota(jnp.int32, (count, LANES), 1) < LANES - shift
    back = (LANES - shift) % LANES
    here = pltpu.roll(summed[layer, pl.ds(down, count), :], back, 1)
    after = pltpu.roll(summed[layer, pl.ds(down + 1, count), :], back, 1)
    result[layer] = jnp.where(low, here, after)


def body(images, cotangent, params, heights, widths):
    grid = Grid(images.shape[1], images.shape[2])
    depth, shard = params.shape
    image_count, row_count = lax.axis_size("img"), lax.axis_size("row")
    count = image_count * row_count
    pixels, width = grid.pixels, images.shape[3]

    small = (shard // UNIT + 2) * TILE
    chunks = -(-shard // UNIT) * TILE
    raw = jnp.pad(params, ((0, 0), (0, chunks * LANES - shard))).reshape(depth, chunks, LANES)

    def parted(stage, first, end, parts=1):
        size = -(-(end - first) // (parts * count * TILE)) * TILE
        return [
            SimpleNamespace(
                stage=stage, name=None, tiles=None, count=1, size=size, lo=start,
                hi=min(start + count * size, end), base=0, start=start,
            )
            for start in range(first, end, count * size)
        ]

    def wire(stage, name, part=0, parts=1):
        start, (rows, columns) = CHUNK[name]
        tiles, rows = columns // LANES, rows // parts
        start += part * rows * tiles
        return SimpleNamespace(
            stage=stage, name=name, tiles=None, count=tiles, size=rows // count, lo=start,
            hi=start + rows * tiles, base=part * rows, start=0,
        )

    wired = all(CHUNK[name][1][0] % (TILE * count) == 0 for name in WIRED)
    if wired:
        spans = [wire(1, WIRED[0]), wire(1, WIRED[1])] + parted(2, PART, GATES_END)
        spans.append(wire(3, WIRED[2]))
        spans.append(
            SimpleNamespace(
                stage=4, name=None, tiles=TILES, count=1, size=TILE, lo=0, hi=0, base=0, start=0
            )
        )
    else:
        spans = parted(1, MIDDLE, BODY_ROWS, 2) + parted(2, PART, MIDDLE) + parted(4, 0, PART)
    margin = max(span.count * span.size for span in spans) + TILE
    sources, shapes, of_name = {}, [], {}
    for index, span in enumerate(spans):
        shapes.append(((span.count, count * span.size, LANES), BF))
        if span.name:
            rows = CHUNK[span.name][1][0]
            of_name[span.name] = SOURCE.format(span.name)
            sources[of_name[span.name]] = ((span.count, rows, LANES), BF)
        elif wired:
            sources[SOURCE.format(index)] = shapes[-1]
    flat_rows = 0 if wired else max(span.lo + count * span.size for span in spans)
    slots_rows = max(flat_rows, count * small)

    def source_of(r, index):
        span = spans[index]
        if span.name:
            return getattr(r, of_name[span.name])
        if wired:
            return getattr(r, SOURCE.format(index))
        return r.slots.at[:, pl.ds(span.start, count * span.size), :]

    late = [
        index for index, span in enumerate(spans) if span.stage >= 3 or span.name == WIRED[1]
    ]

    slots_shape = ((1, slots_rows, LANES), BF)
    field = ((grid.tall * grid.wide * 8, LANES), F32)
    wide = ((pixels, width), F32)
    low = ((pixels, width), BF)
    broad = ((pixels, 4 * width), BF)
    inner = ((pixels, 2 * width), BF)
    narrow_tile = ((pixels, LANES), F32)
    registers = ((pixels * 8, LANES), F32)
    taps = ((49 * 8, LANES), F32)
    taps_grad = ((50 * 8, LANES), F32)
    flat = ((BODY_ROWS, LANES), F32)
    halo = ((grid.halo, width), BF)
    halo_wide = ((grid.halo, 2 * width), BF)
    mask = ((grid.all, LANES), F32)
    own_mask = ((pixels, LANES), F32)
    sum_shape = ((small + 2 * margin, LANES), F32)
    vectors = ((24, 4 * width), F32)
    weights = {name: (PADDED[name], BF) for name in MATRICES}
    kept_one = dict(weights, vectors=vectors, taps=taps, normed=low, field=field)
    kept_two = dict(
        mixed=registers, head=narrow_tile, lines=((pixels, 896), BF), gated=inner,
        branch_a=low, middle=wide, normed_b=low,
    )
    kept_three = dict(active=broad, slope=broad)
    kept_four = dict(branch_b=low)
    front_scratch = dict(
        flat=flat, normed_all=((grid.all, width), BF),
        bias=((8, LANES), F32), x_up=halo, x_down=halo, mask=mask,
    )
    back_scratch = dict(
        grad_up=halo_wide, grad_down=halo_wide, low=low, wide=wide, taps_grad=taps_grad,
        turned=((width, pixels), BF),
    )
    pieces = gather_count(image_count, row_count)
    side = math.isqrt(image_count // 2)
    sum_scratch, sum_sems = {}, {}
    for again, indices in enumerate((range(len(spans)), late)):
        for index in indices:
            parts = Sums.scratch(image_count, row_count, shard, spans[index])
            sum_scratch.update(
                {SUMS.format(index, again, at): shape for at, shape in enumerate(parts)}
            )
            number = Sums.number(image_count, row_count, shard, spans[index])
            sum_sems.update(
                {SENDS.format(index, again): number, RECEIVES.format(index, again): number}
            )
    once = {k: v for k, v in sum_scratch.items() if k.split(DASH)[2] == str(0)}
    once_sems = {k: v for k, v in sum_sems.items() if k.split(DASH)[2] == str(0)}
    turn = ((margin, LANES), F32)

    def summing(r, ring, index, again=0):
        parts = [getattr(r, SUMS.format(index, again, at)) for at in range(6)]
        send = getattr(r, SENDS.format(index, again))
        recv = getattr(r, RECEIVES.format(index, again))
        source = getattr(r, BEFORE.format(index)) if again else source_of(r, index)
        return Sums(ring, source, spans[index], shard, parts, r.turn, send, recv, spans[index].base)

    def wires_of(r):
        return {name: getattr(r, source) for name, source in of_name.items()}

    def settle(r, stage):
        for index, span in enumerate(spans):
            if span.stage == stage and not span.name:
                low = source_of(r, index).at[0]
                if span.tiles:
                    for at, (row, _, _, _) in enumerate(span.tiles):
                        low[at * TILE : (at + 1) * TILE, :] = r.flat[row : row + TILE, :].astype(BF)
                else:
                    narrow(r.flat, low, span.lo, -(-span.hi // TILE) * TILE, span.lo)

    def known(r, ring, beside, stage, target, sums, leave=()):
        settle(r, stage)
        delay, halo = 0.0, (23.5, 19.5, 12.0, 0.0, 0.0)[stage]
        for index, span in enumerate(spans):
            if span.stage == stage and index not in leave:
                part = summing(r, ring, index)
                beside.add(part.steps(target, margin, beside.pace, delay, halo))
                delay += 8 * span.count * span.size * LANES * 2 / beside.pace[0]
                sums.append(part)
        beside.tick(0.0)

    x = images.reshape(pixels, width)
    limits = dict(heights=heights, widths=widths)

    def own_rows(ref):
        return ref.at[pl.ds(grid.halo, pixels), :]

    def kernel_ab(r):
        ring = Ring(image_count, row_count)
        ring.signal(pltpu.get_barrier_semaphore())
        shard_at = (ring.img * row_count + ring.row) * shard
        align_in(shard_at, small, r.raw, r.own, r.flat, 0)
        ring.wait(pltpu.get_barrier_semaphore())
        first = Gather(
            ring, r.own.at[0], r.slots.at[0], small, r.send, r.recv, r.local.at[0], single=True
        )
        first.begin()
        halos = Halo(
            ring, grid, r.x, r.x_up, r.x_down, r.halo_send.at[3], r.halo_recv.at[3]
        )
        halos.begin()
        for layer in range(1, depth):
            align_in(shard_at, small, r.raw, r.own, r.flat, layer)
        fill_mask(grid, ring.row, r.heights, r.widths, r.mask, -3, grid.tall)
        widen = flat_from_slots(count, shard, small, r.slots.at[0], r.flat)
        rest = first.all_single(lambda image, row: widen(image * row_count + row))
        next(rest)
        second = Gather(ring, r.own.at[1], r.slots_b.at[0], small, r.send_b, r.recv_b, r.local.at[1])
        second.begin()
        next(rest, None)
        beside = Steps()
        beside.add(second.steps())
        flat_from_slots(count, shard, small, r.slots.at[0], r.flat, True)
        beside.tick(0.5)
        weights_from_flat(r.flat, r, r.vectors, r.taps, r.bias, beside)
        r.normed = own_rows(r.normed_all)
        forward(grid, r, Vectors(r.vectors), r.taps, r, beside, halos.finish, r.written)
        r.x1[...] = r.result[...]
        r.low[...] = r.result[...].astype(BF)
        halos = Halo(ring, grid, r.low, r.x1_up, r.x1_down, r.halo_send.at[0], r.halo_recv.at[0])
        halos.begin()
        beside.drain()
        second.finish()
        fetch = pltpu.make_async_copy(r.slots_b, r.slots, r.late_sem.at[len(late)])
        fetch.start()
        r.x, r.x_up, r.x_down = r.x1, r.x1_up, r.x1_down
        r.settled()
        fetch.wait()
        beside = Steps()
        loop(count, flat_from_slots(count, shard, small, r.slots.at[0], r.flat))
        flat_from_slots(count, shard, small, r.slots.at[0], r.flat, True)
        weights_from_flat(r.flat, r, r.vectors, r.taps, r.bias, beside)
        r.normed = own_rows(r.normed_all)
        r.mask_own = own_rows(r.mask)
        v = Vectors(r.vectors)
        r.back = r.result
        forward(grid, r, v, r.taps, r, beside, halos.finish, lambda: None)
        r.outputs[...] = r.result[...].astype(BF)
        sums = []
        r.wires = wires_of(r)
        if wired:
            r.grads = r.flat.at[pl.ds(KEPT_ROWS, field[0][0]), :]

        leaving = []

        def leave(stage):
            for at, index in enumerate(late):
                if (spans[index].stage >= 3) == (stage == 4):
                    copy = pltpu.make_async_copy(
                        source_of(r, index), getattr(r, BEFORE.format(index)), r.late_sem.at[at]
                    )
                    copy.start()
                    leaving.append(copy)

        def at_stage(stage):
            def here():
                known(r, ring, beside, stage, r.summed, sums, late)
                if stage == 1:
                    leave(stage)

            return here

        halos = [
            Halo(
                ring, grid, r.gated, r.grad_up, r.grad_down, r.halo_send.at[at], r.halo_recv.at[at],
                (2 - at) * width, width,
            )
            for at in (1, 2)
        ]
        backward_one(
            grid, r, v, r, r.flat, beside, lambda: None, at_stage(0), at_stage(1), halos[0].begin
        )
        halos[1].begin()
        known(r, ring, beside, 2, r.summed, sums)
        backward_two(
            grid, r, v, r.taps, r, r.flat, beside, lambda: None,
            lambda: [halo.finish() for halo in halos], lambda: None, 7,
        )
        settle(r, 4)
        leave(4)
        beside.drain()
        for part in sums:
            part.sent()
        for copy in leaving:
            copy.wait()

    b = call(
        kernel_ab,
        0,
        dict(raw=raw, x=x, grad=cotangent.reshape(pixels, width)),
        dict(outputs=low, input_grad=wide, summed=sum_shape),
        dict(
            kept_one, **kept_two, **kept_three, **kept_four, **front_scratch, **back_scratch,
            **once, **sources, turn=turn, slots=slots_shape, own=((depth, small, LANES), BF),
            result=wide, x1=wide, x1_up=halo, x1_down=halo, **({} if wired else dict(grads=field)),
        ),
        dict(
            once_sems, send=pieces, recv=pieces, send_b=pieces, recv_b=pieces, local=2,
            halo_send=(4, 2), halo_recv=(4, 2), late_sem=len(late) + 1,
        ),
        limits,
        spilled=(kept_one, kept_two, kept_three, kept_four),
        placed=dict({BEFORE.format(index): shapes[index] for index in late}, slots_b=slots_shape),
    )
    a = b

    def kernel_c(r):
        ring = Ring(image_count, row_count)
        ring.signal(pltpu.get_barrier_semaphore())
        fill_mask(grid, ring.row, r.heights, r.widths, r.mask_own, 0, grid.rows)
        r.both[1] = r.summed[...]
        ring.wait(pltpu.get_barrier_semaphore())
        v = Vectors(r.vectors)
        beside = Steps((LAST_LINK, LAST_HOP))
        r.needed()
        sums = []

        def late_sums(last):
            delay = 0.0
            for index in late[::-1]:
                if (spans[index].stage >= 3) == last:
                    before = summing(r, ring, index, 1)
                    beside.add(before.steps(r.both.at[1], margin, beside.pace, delay))
                    sums.append(before)
                    delay += 4 * spans[index].count * spans[index].size * LANES * 2 / beside.pace[0]
            beside.tick(0.0)

        late_sums(True)
        target = r.both.at[0]
        r.back = r.grad
        r.wires = wires_of(r)

        def at_stage(stage):
            return lambda: known(r, ring, beside, stage, target, sums)

        halos = [
            Halo(
                ring, grid, r.gated, r.grad_up, r.grad_down, r.halo_send.at[at], r.halo_recv.at[at],
                (1 - at) * width, width,
            )
            for at in (0, 1)
        ]

        def half_here():
            r.needed()
            late_sums(False)
            known(r, ring, beside, 0, target, sums)

        backward_one(
            grid, r, v, r, r.flat, beside, r.needed, half_here, at_stage(1), halos[0].begin
        )
        halos[1].begin()
        known(r, ring, beside, 2, target, sums)
        backward_two(
            grid, r, v, r.taps, r, r.flat, beside, r.needed,
            lambda: [halo.finish() for halo in halos], at_stage(3), 4,
        )
        known(r, ring, beside, 4, target, sums)
        start = (ring.img * row_count + ring.row) * shard
        beside.drain(lambda: align_out(start, margin, r.both, r.grads_out, 1))
        align_out(start, margin, r.both, r.grads_out, 0)
        for part in sums:
            part.sent()

    late_parts = [
        {
            BEFORE.format(index): getattr(b, BEFORE.format(index))
            for index in late
            if (spans[index].stage >= 3) == last
        }
        for last in (False, True)
    ]
    c = call(
        kernel_c,
        2,
        dict(x=x, summed=b.summed),
        dict(input_grad=low, grads_out=((depth, chunks, LANES), F32)),
        dict(
            **back_scratch, **sum_scratch, **sources, turn=turn, grads=field,
            flat=((KEPT_ROWS if wired else BODY_ROWS, LANES), F32),
            **({} if wired else dict(slots=((1, flat_rows, LANES), BF))),
            mask_own=own_mask, both=((depth, small + 2 * margin, LANES), F32),
        ),
        dict(sum_sems, halo_send=(2, 2), halo_recv=(2, 2)),
        limits,
        fetched=(
            dict(late_parts[1], grad=b.input_grad, vectors=a.vectors, branch_b=a.branch_b),
            dict(reduce=a.reduce, active=a.active, slope=a.slope, normed_b=a.normed_b),
            late_parts[0],
            dict(expand=a.expand, middle=a.middle, branch_a=a.branch_a),
            dict(outer_weight=a.outer_weight, gated=a.gated, lines=a.lines, mixed=a.mixed, head=a.head,
                 order_one=a.order_one, order_two=a.order_two, order_three=a.order_three),
            dict(field=a.field, taps=a.taps, normed=a.normed, inner_weight=a.inner_weight),
        ),
    )
    summed = c.grads_out.reshape(depth, -1)[:, :shard]
    return (b.outputs.reshape(images.shape), c.input_grad.reshape(images.shape), summed)


def solution(mesh):
    return jax.shard_map(
        body,
        mesh=mesh,
        in_specs=(
            P("img", "row", None, None),
            P("img", "row", None, None),
            P(None, ("img", "row")),
            P("img"),
            P("img"),
        ),
        out_specs=(
            P("img", "row", None, None),
            P("img", "row", None, None),
            P(None, ("img", "row")),
        ),
        check_vma=False,
    )
```

time: 1570 us -> 247 us (0.16); the launches traced: 1550 us -> 247 us
  local copies, waits for them, and re-layouts: 682 us -> 6.46 us
  other arithmetic: 452 us -> 0 us
  waiting for transfers between devices: 309 us -> 0 us
  Pallas kernels: 0 us -> 238 us
  matrix products: 53.8 us -> 0 us
  starting transfers between devices: 34.5 us -> 0 us
  between operations: 21.2 us -> 1.96 us
    unnamed x4 -> x0, waiting for transfers between devices: 297 us -> none
    reduce_sum x29 -> x0, other arithmetic: 255 us -> none  [the longest x2 210 us: body(): partial_sum = jnp.sum(received, 0)]
    pallas_call x0 -> x2, Pallas kernels: none -> 238 us  [call(): pl.pallas_call(run, out_shape=[jax.ShapeDtypeStruct(*shape) for shape in...]
    unnamed x617 -> x9, local copies, waits for them, and re-layouts: 222 us -> 5.54 us
    concatenate x2 -> x0, local copies, waits for them, and re-layouts: 190 us -> none  [layer_back(): return (grad_values, jnp.concatenate(flat_pieces))]
    slice x25 -> x1, local copies, waits for them, and re-layouts: 177 us -> 0.93 us  [body(): summed = c.grads_out.reshape(depth, -1)[:, :shard]]
    convert_element_type x21 -> x0, other arithmetic: 121 us -> none  [the longest x2 83 us: body(): flat.reshape(image_count, -1).astype(jnp.bfloat16)]
    dot_general x42 -> x0, matrix products: 53.8 us -> none  [the longest x14 22.7 us: back_product(): lax.dot_general(grad, weight, (((grad.ndim - 1,), (1,)), ((), ())), prefe...]
  transfers between devices with their start and end apart: 12 -> 0, of which waited for: 4 -> 0; matrix products, arithmetic and copies ran while one was open for 33% -> 0% of each run, Pallas kernels for 0% -> 0%
where the time goes in v1:
time: 247 us
  Pallas kernels  238 us (96%)
  local copies, waits for them, and re-layouts  6.46 us (3%)
    pallas_call x2, Pallas kernels, call(): pl.pallas_call(run, out_shape=[jax.ShapeDtypeStruct(*shape) for shape in...  238 us
    unnamed x9, local copies, waits for them, and re-layouts  5.54 us

profile of v1, /device:TPU:0, one launch (start us, length us, event | category | flops | bytes accessed | tf_op | source)
XLA Modules:
  0.0 246.5 jit_solution(12076071835702468524)
XLA Ops:
  1.9 1.3 pad_bitcast_fusion
  3.3 0.8 copy.13
  4.1 155.3 %shard_map.76 = (bf16[480,512]{1,0:T(8,128)(2,1)}, f32[480,512]{1,0:T(8,128)}, f32[1328,128]{1,0:T(8,128)}, bf16[512,1024]{1,0:T(8,128)(2,1)}, bf16[128,128]{1,0...) custom-call(bf16[2,768,128]{2,1,0:T(8,128)(2,1)} %bitcast.16, ...), custom_call_target="tpu_custom_call" | custom-call | tf_op jit(solution)/shard_map/pallas_call | solution.py:1372
  159.4 82.8 %shard_map.77 = (bf16[480,512]{1,0:T(8,128)(2,1)}, f32[2,768,128]{2,1,0:T(8,128)}) custom-call(bf16[480,512]{1,0:T(8,128)(2,1)} %bitcast.15, f32[1328,128]{1,0:T(8,128)} %get-tuple-element.33.refs_1_, s32[1]{0:T(128)S(6)} %copy.16.refs_3_.refs_2_, s32[1]{0:T(128)S(6)} %copy.17.refs_4_.refs_3_, bf16[8,512,128]{2,1,0:T(8,128)(2,1)} %get-tuple-element.34.refs_4_, ...), custom_call_target="tpu_custom_call" | custom-call | tf_op jit(solution)/shard_map/pallas_call | solution.py:1372
  242.2 0.0 copy-start
  242.2 0.0 copy-start.1
  242.2 1.8 copy.12
  244.0 0.9 slice.4
  245.0 0.0 copy-done
  245.0 0.8 copy.18
  245.8 0.0 copy-done.1
  245.8 0.8 copy.19
Async XLA Ops:
  242.2 2.8 %copy-start = (bf16[480,512]{1,0:T(8,128)(2,1)S(1)}, bf16[480,512]{1,0:T(8,128)(2,1)}, u32[]{:S(2)}) copy-start(bf16[480,512]{1,0:T(8,128)(2,1)} %get-tuple-element.32) | copy-start | bytes 1474564
  242.2 3.5 %copy-start.1 = (bf16[480,512]{1,0:T(8,128)(2,1)S(1)}, bf16[480,512]{1,0:T(8,128)(2,1)}, u32[]{:S(2)}) copy-start(bf16[480,512]{1,0:T(8,128)(2,1)} %get-tuple-element.59) | copy-start | bytes 1474564
